TPU v7x, 32 devices: a whole 2x2x4 slice. The times are simulated.
32 devices in a mesh: pairs: 16 (over z, y, x), heads: 2 (over core).
Axes of the slice: x: 2, y: 2, z: 4, core: 2. Of those that a mesh axis runs over, the one named last changes fastest.
Arguments:
- tokens: bfloat16 [64, 280, 768], P(('pairs', 'heads')), may hold values from -6 to 6
- cotangent: bfloat16 [64, 280, 768], P(('pairs', 'heads')), may hold values from -6 to 6
- text_len: int32 [64], P('pairs'), may hold values from 6 to 40, as said below
- word_mask: int32 [64, 40], P(('pairs', 'heads')), may hold values from 0 to 1, as said below
- attn_gain: float32 [768], replicated, may hold values from 0.1 to 1.9
- attn_shift: float32 [768], replicated, may hold values from -1.5 to 1.5
- w_qkv: bfloat16 [3, 768, 768], P(None, None, 'heads'), may hold values from -0.21875 to 0.21875
- qv_bias: float32 [2, 768], P(None, 'heads'), may hold values from -2.5 to 2.5
- w_out: bfloat16 [768, 768], replicated, may hold values from -0.875 to 0.875
- out_bias: float32 [768], replicated, may hold values from -1.5 to 1.5
- mlp_gain: float32 [768], replicated, may hold values from 0.1 to 1.9
- mlp_shift: float32 [768], replicated, may hold values from -1.5 to 1.5
- w_up: bfloat16 [768, 3072], P(None, 'heads'), may hold values from -0.21875 to 0.21875
- up_bias: bfloat16 [3072], P('heads'), may hold values from -2.5 to 2.5
- w_down: bfloat16 [3072, 768], P('heads'), may hold values from -0.109375 to 0.109375
- down_bias: float32 [768], replicated, may hold values from -1.5 to 1.5
Outputs:
- layer_out: bfloat16 [64, 280, 768], P(('pairs', 'heads'))
- grad_tokens: float32 [64, 280, 768], P(('pairs', 'heads'))
- grad_attn_gain: float32 [768], P(('pairs', 'heads'))
- grad_attn_shift: float32 [768], P(('pairs', 'heads'))
- grad_w_qkv: float32 [3, 768, 768], P(None, 'pairs', 'heads')
- grad_qv_bias: float32 [2, 768], P(None, ('pairs', 'heads'))
- grad_w_out: float32 [768, 768], P(('pairs', 'heads'))
- grad_out_bias: float32 [768], P(('pairs', 'heads'))
- grad_mlp_gain: float32 [768], P(('pairs', 'heads'))
- grad_mlp_shift: float32 [768], P(('pairs', 'heads'))
- grad_w_up: float32 [768, 3072], P('pairs', 'heads')
- grad_up_bias: float32 [3072], P(('pairs', 'heads'))
- grad_w_down: float32 [3072, 768], P('heads', 'pairs')
- grad_down_bias: float32 [768], P(('pairs', 'heads'))
Inputs may be any that keep to these rules, and one draw needn't show every extreme that they name: `text_len`: every caption has 6 to 40 live word slots; some caption has 40. `word_mask`: 1 only at word slots below the caption's text_len; the number of masked slots varies widely from caption to caption.
All inputs are finite; a program needn't handle non-finite values.
Results may differ from a plain program's by a relative error of at most 0.014.
Values may be sent and summed in bfloat16 or wider, within the bound.
No kernel may reach another device: no remote copies, remote signals or barrier semaphores. Data moves between devices by JAX's collectives and lax.ppermute only.
A program may use at most 192 MiB of HBM per device.

v0:
```python
import math

import jax
import jax.numpy as jnp
from jax import lax
from jax.sharding import PartitionSpec as P

HEAD_DIM = 64
WORDS = 40


epsilon = 1e-06
masked_score = -1000000000.0


def norm_fwd(rows, gain_vec, shift_vec):
    mean_val = jnp.mean(rows, axis=-1, keepdims=True)
    centred = rows - mean_val
    inv_std = lax.rsqrt(jnp.mean(centred * centred, axis=-1, keepdims=True) + epsilon)
    unit_rows = centred * inv_std
    return (unit_rows * gain_vec + shift_vec, unit_rows, inv_std)


def norm_back(grad_rows, unit_rows, inv_std, gain_vec):
    scaled = grad_rows * gain_vec
    first = jnp.mean(scaled, axis=-1, keepdims=True)
    second = jnp.mean(scaled * unit_rows, axis=-1, keepdims=True)
    grad_in = inv_std * (scaled - first - unit_rows * second)
    return (grad_in, jnp.sum(grad_rows * unit_rows, axis=(0, 1)), jnp.sum(grad_rows, axis=(0, 1)))


def gelu_slope(values_in):
    cumulative = 0.5 * (1.0 + lax.erf(values_in * 0.7071067811865476))
    density = jnp.exp(-0.5 * values_in * values_in) * 0.3989422804014327
    return cumulative + values_in * density


def per_device(
    tokens,
    cotangent,
    text_len,
    word_mask,
    attn_gain,
    attn_shift,
    w_qkv,
    qv_bias,
    w_out,
    out_bias,
    mlp_gain,
    mlp_shift,
    w_up,
    up_bias,
    w_down,
    down_bias,
):
    local_pairs, seq_len, width = tokens.shape
    local_width = w_qkv.shape[2]
    local_heads = local_width // HEAD_DIM
    scale = 1.0 / math.sqrt(HEAD_DIM)
    zero_index = jnp.zeros((), jnp.int32)
    head_index = lax.axis_index("heads")
    tok_rows = tokens.astype(jnp.float32)
    normed, unit_one, inv_one = norm_fwd(tok_rows, attn_gain, attn_shift)
    normed_low = normed.astype(jnp.bfloat16)
    normed_all = lax.all_gather(normed_low, "heads", axis=0, tiled=True)
    group_pairs = normed_all.shape[0]
    proj = jnp.einsum("nsd,tdc->tnsc", normed_all, w_qkv, preferred_element_type=jnp.float32)
    head_shape = (group_pairs, seq_len, local_heads, HEAD_DIM)
    queries = (proj[0] + qv_bias[0]).astype(jnp.bfloat16).reshape(head_shape)
    key_rows = proj[1].astype(jnp.bfloat16).reshape(head_shape)
    values = (proj[2] + qv_bias[1]).astype(jnp.bfloat16).reshape(head_shape)
    position = jnp.arange(seq_len, dtype=jnp.int32)
    key_ok = (position[None, :] >= WORDS) | (position[None, :] < text_len[:, None])

    def score_rows():
        raw = (
            jnp.einsum("nqhe,nkhe->nhqk", queries, key_rows, preferred_element_type=jnp.float32)
            * scale
        )
        return jnp.where(key_ok[:, None, None, :], raw, masked_score)

    scores = score_rows()
    row_max = jnp.max(scores, axis=-1, keepdims=True)
    weights = jnp.exp(scores - row_max)
    total = jnp.sum(weights, axis=-1, keepdims=True)
    log_total = row_max + jnp.log(total)
    probs_low = (weights / total).astype(jnp.bfloat16)
    context = jnp.einsum("nhqk,nkhe->nqhe", probs_low, values, preferred_element_type=jnp.float32)
    context = context.reshape(group_pairs, seq_len, local_width).astype(jnp.bfloat16)
    context_tok = lax.all_to_all(context, "heads", split_axis=0, concat_axis=2, tiled=True)
    attn_out = (
        jnp.einsum("nsc,cd->nsd", context_tok, w_out, preferred_element_type=jnp.float32) + out_bias
    )
    resid = tok_rows + attn_out
    mlp_norm, unit_two, inv_two = norm_fwd(resid, mlp_gain, mlp_shift)
    mlp_low = mlp_norm.astype(jnp.bfloat16)
    keep = jnp.concatenate(
        [word_mask.astype(jnp.float32), jnp.ones((local_pairs, seq_len - WORDS), jnp.float32)],
        axis=1,
    )
    grad_final = cotangent.astype(jnp.float32) * keep[:, :, None]
    grad_mlp_low = grad_final.astype(jnp.bfloat16)
    grad_down_bias = jnp.sum(grad_mlp_low.astype(jnp.float32), axis=(0, 1))
    up_full, down_full, up_bias_full = (
        lax.all_gather(w_up, "heads", axis=1, tiled=True),
        lax.all_gather(w_down, "heads", axis=0, tiled=True),
        lax.all_gather(up_bias, "heads", axis=0, tiled=True),
    )
    hidden_pre = jnp.einsum(
        "nsd,df->nsf", mlp_low, up_full, preferred_element_type=jnp.float32
    ) + up_bias_full.astype(jnp.float32)
    act_low = jax.nn.gelu(hidden_pre, approximate=False).astype(jnp.bfloat16)
    mlp_out = (
        jnp.einsum("nsf,fd->nsd", act_low, down_full, preferred_element_type=jnp.float32)
        + down_bias
    )
    layer_out = (resid + mlp_out).astype(jnp.bfloat16)
    down_term_grad = jnp.einsum(
        "nsf,nsd->fd", act_low, grad_mlp_low, preferred_element_type=jnp.float32
    )
    grad_act = jnp.einsum(
        "nsd,fd->nsf", grad_mlp_low, down_full, preferred_element_type=jnp.float32
    )
    grad_pre = (grad_act * gelu_slope(hidden_pre)).astype(jnp.bfloat16)
    up_term_grad = jnp.einsum("nsd,nsf->df", mlp_low, grad_pre, preferred_element_type=jnp.float32)
    up_bias_term = jnp.sum(grad_pre.astype(jnp.float32), axis=(0, 1))
    grad_mlp_in = jnp.einsum("nsf,df->nsd", grad_pre, up_full, preferred_element_type=jnp.float32)
    grad_resid_norm, grad_mlp_gain, grad_mlp_shift = norm_back(
        grad_mlp_in, unit_two, inv_two, mlp_gain
    )
    grad_resid = grad_final + grad_resid_norm
    grad_attn_low = grad_resid.astype(jnp.bfloat16)
    grad_w_out = jnp.einsum(
        "nsc,nsd->cd", context_tok, grad_attn_low, preferred_element_type=jnp.float32
    )
    grad_out_bias = jnp.sum(grad_attn_low.astype(jnp.float32), axis=(0, 1))
    grad_context = jnp.einsum(
        "nsd,cd->nsc", grad_attn_low, w_out, preferred_element_type=jnp.float32
    ).astype(jnp.bfloat16)
    grad_context_heads = lax.all_to_all(
        grad_context, "heads", split_axis=2, concat_axis=0, tiled=True
    ).reshape(head_shape)
    probs = jnp.exp(score_rows() - log_total)
    probs_again = probs.astype(jnp.bfloat16)
    grad_values = jnp.einsum(
        "nhqk,nqhe->nkhe", probs_again, grad_context_heads, preferred_element_type=jnp.float32
    ).astype(jnp.bfloat16)
    grad_probs = jnp.einsum(
        "nqhe,nkhe->nhqk", grad_context_heads, values, preferred_element_type=jnp.float32
    )
    inner_sum = jnp.sum(probs * grad_probs, axis=-1, keepdims=True)
    grad_scores = (probs * (grad_probs - inner_sum)).astype(jnp.bfloat16)
    grad_queries = (
        scale
        * jnp.einsum("nhqk,nkhe->nqhe", grad_scores, key_rows, preferred_element_type=jnp.float32)
    ).astype(jnp.bfloat16)
    grad_keys = (
        scale
        * jnp.einsum("nhqk,nqhe->nkhe", grad_scores, queries, preferred_element_type=jnp.float32)
    ).astype(jnp.bfloat16)
    flat_shape = (group_pairs, seq_len, local_width)
    grad_proj = jnp.stack(
        [
            grad_queries.reshape(flat_shape),
            grad_keys.reshape(flat_shape),
            grad_values.reshape(flat_shape),
        ],
        axis=1,
    )
    grad_qkv_local = jnp.einsum(
        "nsd,ntsc->tdc", normed_all, grad_proj, preferred_element_type=jnp.float32
    )
    bias_local = jnp.stack(
        [
            jnp.sum(grad_proj[:, 0].astype(jnp.float32), axis=(0, 1)),
            jnp.sum(grad_proj[:, 2].astype(jnp.float32), axis=(0, 1)),
        ],
        axis=0,
    )
    qv_term = lax.dynamic_update_slice(
        jnp.zeros((2, width), jnp.float32), bias_local, (zero_index, head_index * local_width)
    )
    grad_normed = lax.psum_scatter(
        jnp.einsum("ntsc,tdc->nsd", grad_proj, w_qkv, preferred_element_type=jnp.float32).astype(
            jnp.bfloat16
        ),
        "heads",
        scatter_dimension=0,
        tiled=True,
    ).astype(jnp.float32)
    grad_tok_norm, grad_attn_gain, grad_attn_shift = norm_back(
        grad_normed, unit_one, inv_one, attn_gain
    )
    grad_tokens = grad_resid + grad_tok_norm
    up_term_grad, down_term_grad = (
        lax.psum_scatter(
            up_term_grad.astype(jnp.bfloat16), "heads", scatter_dimension=1, tiled=True
        ).astype(jnp.float32),
        lax.psum_scatter(
            down_term_grad.astype(jnp.bfloat16), "heads", scatter_dimension=0, tiled=True
        ).astype(jnp.float32),
    )
    grad_w_qkv, grad_w_up, grad_w_down = (
        lax.psum_scatter(grad_qkv_local, "pairs", scatter_dimension=1, tiled=True),
        lax.psum_scatter(up_term_grad, "pairs", scatter_dimension=0, tiled=True),
        lax.psum_scatter(down_term_grad, "pairs", scatter_dimension=1, tiled=True),
    )
    summed = (
        lax.psum_scatter(grad_w_out, ("pairs", "heads"), scatter_dimension=0, tiled=True),
        lax.psum_scatter(grad_attn_gain, ("pairs", "heads"), scatter_dimension=0, tiled=True),
        lax.psum_scatter(grad_attn_shift, ("pairs", "heads"), scatter_dimension=0, tiled=True),
        lax.psum_scatter(grad_out_bias, ("pairs", "heads"), scatter_dimension=0, tiled=True),
        lax.psum_scatter(grad_mlp_gain, ("pairs", "heads"), scatter_dimension=0, tiled=True),
        lax.psum_scatter(grad_mlp_shift, ("pairs", "heads"), scatter_dimension=0, tiled=True),
        lax.psum_scatter(up_bias_term, ("pairs", "heads"), scatter_dimension=0, tiled=True),
        lax.psum_scatter(grad_down_bias, ("pairs", "heads"), scatter_dimension=0, tiled=True),
        lax.psum_scatter(qv_term, ("pairs", "heads"), scatter_dimension=1, tiled=True),
    )
    return (
        layer_out,
        grad_tokens,
        summed[1],
        summed[2],
        grad_w_qkv,
        summed[8],
        summed[0],
        summed[3],
        summed[4],
        summed[5],
        grad_w_up,
        summed[6],
        grad_w_down,
        summed[7],
    )


def solution(mesh):
    in_specs = (
        P(("pairs", "heads"), None, None),
        P(("pairs", "heads"), None, None),
        P("pairs"),
        P(("pairs", "heads"), None),
        P(),
        P(),
        P(None, None, "heads"),
        P(None, "heads"),
        P(),
        P(),
        P(),
        P(),
        P(None, "heads"),
        P("heads"),
        P("heads", None),
        P(),
    )
    out_specs = (
        P(("pairs", "heads"), None, None),
        P(("pairs", "heads"), None, None),
        P(("pairs", "heads")),
        P(("pairs", "heads")),
        P(None, "pairs", "heads"),
        P(None, ("pairs", "heads")),
        P(("pairs", "heads"), None),
        P(("pairs", "heads")),
        P(("pairs", "heads")),
        P(("pairs", "heads")),
        P("pairs", "heads"),
        P(("pairs", "heads")),
        P("heads", "pairs"),
        P(("pairs", "heads")),
    )
    return jax.shard_map(
        per_device, mesh=mesh, in_specs=in_specs, out_specs=out_specs, check_vma=False
    )
```

profile of v0, /device:TPU:0, one launch (start us, length us, event | category | flops | bytes accessed | tf_op | source)
XLA Modules:
  0.0 778.1 jit_solution(3410052084191913099)
XLA Ops:
  7.2 1.5 convert_reduce_fusion.2
  8.7 1.5 fusion.43
  10.9 2.5 fusion.39
  13.5 0.7 all-gather.7.cloned.1.call-update
  14.2 0.7 all-gather.9.cloned.1.call-update
  15.2 1.9 all-gather
  17.8 8.5 %all-gather.5.cloned.1.call-done = bf16[4,280,768]{2,1,0:T(8,128)(2,1)} async-done(((bf16[2,280,768]{2,1,0:T(8,128)(2,1)}), bf16[4,280,768]{2,1,0:T(8,128)(2,1)}) %all-gather.5.cloned.1.call-update) | async-done | bytes 1720336 | tf_op jit(solution)/shard_map/all_gather | solution.py:65
  26.3 3.9 convolution_bitcast_fusion
  30.2 1.0 slice.27
  31.2 2.1 fusion.72
  33.2 1.6 copy.63
  34.9 3.5 copy.61
  38.4 3.1 copy.62
  41.5 4.7 fusion.28
  46.2 2.6 fusion
  48.8 1.6 copy-done.1
  50.5 4.1 fusion.51
  54.6 1.8 copy.65
  56.4 4.8 all_to_all.33
  61.2 0.7 copy.89
  61.9 1.4 all_to_all.27
  63.4 2.5 fusion.73
  65.9 1.2 copy-done.9
  67.5 7.8 %fusion.50 = (u8[280,3072]{1,0:T(8,128)(4,1)S(1)}, u8[280,3072]{1,0:T(8,128)(4,1)S(1)}, f32[2,280,3072]{2,1,0:T(8,128)S(1)}) fusion(f32[3072]{0:T(1024)S(1)} %bitcast.111, bf16[768,3072]{1,0:T(8,128)(2,1)} %all-gather.7.cloned.1.call-done, f32[2,280,768]{2,1,0:T(8,128)} %copy-done.9, f32[768]{0:T(1024)S(1)} %copy-done.49, f32[768]{0:T(1024)S(1)} %copy-done.38, ...), kind=kOutput, calls=%fused_computation.98 | convolution fusion | flops 2666926080 | bytes 15063424 | tf_op jit(solution)/shard_map/nsd,df->nsf/dot_general | solution.py:109
  75.3 16.2 %fusion.4 = bf16[2,280,3072]{2,1,0:T(8,128)(2,1)S(1)} fusion(f32[2,280,3072]{2,1,0:T(8,128)S(1)} %get-tuple-element.85, f32[3072]{0:T(1024)S(1)} %bitcast.112, u8[280,3072]{1,0:T(8,128)(4,1)S(1)} %get-tuple-element.57, u8[280,3072]{1,0:T(8,128)(4,1)S(1)} %get-tuple-element.56), kind=kLoop, calls=%fused_computation.14 | loop fusion | flops 122142720 | bytes 12054528 | tf_op jit(solution)/shard_map/convert_element_type | solution.py:112
  91.5 1.7 copy-done.13
  93.3 5.9 bitcast_convert_fusion
  99.4 8.5 %convert_reduce_fusion = (f32[3072]{0:T(1024)}, bf16[2,280,3072]{2,1,0:T(8,128)(2,1)S(1)}) fusion(f32[2,280,3072]{2,1,0:T(8,128)} %copy-done.7, f32[3072]{0:T(1024)S(1)} %bitcast.113, bf16[3072,768]{1,0:T(8,128)(2,1)} %all-gather.9.cloned.1.call-done, bf16[2,280,768]{2,1,0:T(8,128)(2,1)S(1)} %copy-done.14, f32[2,280]{1,0:T(2,128)} %concatenate.3), kind=kOutput, calls=%fused_computation.26 | convolution fusion | flops 2666062848 | bytes 15927488 | tf_op jit(solution)/shard_map/nsd,fd->nsf/dot_general | solution.py:121
  107.9 2.1 copy-done.53
  110.0 5.9 bitcast_convert_fusion.1
  116.0 1.4 log_add_fusion
  117.5 7.8 %multiply_reduce_fusion.1 = (f32[768]{0:T(1024)}, f32[2,280]{1,0:T(2,128)S(1)}, f32[2,280]{1,0:T(2,128)S(1)}, f32[768]{0:T(1024)}, f32[2,280,768]{2,1,0:T(8,128)S(1)}) fusion(f32[2,280,768]{2,1,0:T(8,128)} %copy-done.9, f32[2,280]{1,0:T(2,128)S(1)} %copy-done.35, f32[2,280]{1,0:T(2,128)S(1)} %copy-done.27, f32[768]{0:T(1024)} %param.26, ...), kind=kOutput, calls=%fused_computation.88 | convolution fusion | flops 2646279680 | bytes 11618048 | tf_op jit(solution)/shard_map/nsf,df->nsd/dot_general | solution.py:127
  125.3 1.4 convert_reduce_fusion.6
  126.8 1.2 copy-done.8
  128.0 0.9 convolution_convert_fusion
  128.9 2.8 copy.67
  131.7 6.0 all_to_all.34
  137.9 8.6 %convert_reduce_fusion.3 = (f32[6,64]{1,0:T(8,128)}, bf16[4,6,64,280]{3,2,1,0:T(8,128)(2,1)}) fusion(bf16[4,280,6,64]{1,3,2,0:T(8,128)(2,1)S(1)} %bitcast.102, f32[4,6,280]{2,1,0:T(8,128)S(1)} %copy-done.16, f32[4,6,280,280]{2,3,1,0:T(8,128)} %copy-done.1, pred[4,280]{1,0:T(4,128)(4,1)S(1)} %copy-done.21), kind=kOutput, calls=%fused_computation.63 | convolution fusion | flops 249661056 | bytes 9276256 | tf_op jit(solution)/shard_map/nhqk,nqhe->nkhe/dot_general | solution.py:145
  146.5 1.6 copy.74
  148.1 9.5 %multiply_reduce_fusion = (f32[4,6,280]{2,1,0:T(8,128)S(1)}, f32[4,6,280,280]{2,3,1,0:T(8,128)S(1)}) fusion(f32[4,6,280]{2,1,0:T(8,128)S(1)} %copy-done.16, f32[4,6,280,280]{2,3,1,0:T(8,128)} %copy-done.1, pred[4,280]{1,0:T(4,128)(4,1)S(1)} %copy-done.21, bf16[4,280,6,64]{1,3,2,0:T(8,128)(2,1)} %bitcast.103, f32[4,280,6,64]{1,3,2,0:T(8,128)} %bitcast.100, ...), kind=kOutput, calls=%fused_computation.1 | convolution fusion | flops 251106240 | bytes 17689696 | tf_op jit(solution)/shard_map/nqhe,nkhe->nhqk/dot_general | solution.py:148
  157.6 6.2 multiply_convert_fusion
  163.8 2.6 convert_reduce_fusion.4
  166.5 2.3 copy.72
  168.8 6.2 multiply_convert_fusion.1
  175.0 2.5 copy.73
  177.5 5.1 bitcast_convert_fusion.2
  182.7 6.5 convolution_bitcast_fusion.1
  189.1 6.5 copy.75
  195.7 1.1 copy-done.15
  196.8 4.0 convolution_bitcast_fusion.2
  200.9 4.7 copy.86
  205.6 5.2 convert_element_type.153
  210.9 0.6 copy-done.52
  213.0 7.7 add_convert_fusion.2
  220.7 2.1 fusion.45
  222.8 43.3 %all-reduce.10 = (f32[768]{0:T(1024)S(1)}, f32[768]{0:T(1024)S(1)}, f32[2,768]{1,0:T(2,128)S(1)}, f32[768]{0:T(1024)S(1)}, f32[768]{0:T(1024)S(1)}, /*index=5*/f...) all-reduce(f32[768]{0:T(1024)S(1)} %get-tuple-element.60, ...), channel_id=3, replica_groups=mesh['pairs'=16,'heads'=2] {'pairs','heads'}, use_global_device_ids=true, to_apply=%region_13.14.clone | all-reduce | flops 9216 | bytes 73728
  270.2 0.6 constant_dynamic-slice_fusion
  270.8 3.5 fusion.42
  274.4 107.7 %all-reduce.13.cloned.1.call-done = f32[3,768,384]{2,0,1:T(4,128)} async-done(((f32[3,768,384]{2,0,1:T(4,128)}), f32[3,768,384]{2,0,1:T(4,128)}) %all-reduce.13.cloned.1.call-update) | async-done | bytes 3538960
  382.0 1.0 constant_dynamic-slice_fusion.1
  383.1 0.7 copy.76
  383.8 102.2 %reduce-scatter.12.cloned.1.call-done = f32[24,768]{1,0:T(8,128)} async-done(((f32[768,768]{1,0:T(8,128)}), f32[24,768]{1,0:T(8,128)}) %reduce-scatter.12.cloned.1.call-update) | async-done | bytes 73744 | tf_op jit(solution)/shard_map/reduce_scatter | solution.py:209
  486.0 143.1 %reduce-scatter.20.cloned.1.call-done = f32[48,1536]{1,0:T(8,128)} async-done(((f32[768,1536]{1,0:T(8,128)}), f32[48,1536]{1,0:T(8,128)}) %reduce-scatter.20.cloned.1.call-update) | async-done | bytes 294928
  629.1 141.7 %reduce-scatter.16.cloned.1.call-done = f32[48,1536]{1,0:T(8,128)} async-done(((f32[768,1536]{1,0:T(8,128)}), f32[48,1536]{1,0:T(8,128)}) %reduce-scatter.16.cloned.1.call-update) | async-done | bytes 294928 | tf_op jit(solution)/shard_map/reduce_scatter | solution.py:205
  (154 shorter events, 7.8 us)
Async XLA Ops:
  7.2 19.1 %copy-start = (bf16[3,768,384]{2,1,0:T(8,128)(2,1)S(1)}, bf16[3,768,384]{2,1,0:T(8,128)(2,1)}, u32[]{:S(2)}) copy-start(bf16[3,768,384]{2,1,0:T(8,128)(2,1)} %param.22) | copy-start | bytes 5308420
  7.2 19.1 %all-gather.5.cloned.1.call-start = ((), (), s32[]{:S(2)}) async-start(), calls=%async_computation.8 | async-start | bytes 2580480 | tf_op jit(solution)/shard_map/all_gather | solution.py:65
  10.3 0.6 copy-start.18
  10.9 4.1 copy-start.46
  10.9 4.1 copy-start.45
  10.9 4.3 copy-start.41
  10.9 6.3 copy-start.47
  13.4 54.0 %all-gather.7.cloned.1.call-start = ((), (), s32[]{:S(2)}) async-start(), calls=%async_computation.9 | async-start | bytes 7077888 | tf_op jit(solution)/shard_map/all_gather | solution.py:105
  14.2 85.2 %all-gather.9.cloned.1.call-start = ((), (), s32[]{:S(2)}) async-start(), calls=%async_computation.10 | async-start | bytes 7077888 | tf_op jit(solution)/shard_map/all_gather | solution.py:106
  14.9 186.0 %reduce-scatter.18.cloned.1.call-start = ((), (), s32[]{:S(2)}) async-start(), calls=%async_computation.15 | async-start | bytes 7077888 | tf_op jit(solution)/shard_map/reduce_scatter | solution.py:199
  15.1 33.7 %copy-start.28 = (f32[6,64]{1,0:T(8,128)}, f32[6,64]{1,0:T(8,128)S(1)}, u32[]{:S(2)}) copy-start(f32[6,64]{1,0:T(8,128)S(1)} %add.142) | copy-start | bytes 4612
  15.2 26.3 %copy-start.23 = (f32[6,64]{1,0:T(8,128)}, f32[6,64]{1,0:T(8,128)S(1)}, u32[]{:S(2)}) copy-start(f32[6,64]{1,0:T(8,128)S(1)} %add.145) | copy-start | bytes 4612
  17.2 31.6 %copy-start.20 = (pred[4,280]{1,0:T(4,128)(4,1)}, pred[4,280]{1,0:T(4,128)(4,1)S(1)}, u32[]{:S(2)}) copy-start(pred[4,280]{1,0:T(4,128)(4,1)S(1)} %fusion.63) | copy-start | bytes 3364
  34.9 6.6 copy-start.4
  46.2 4.3 copy-start.1
  46.2 4.3 copy-start.6
  48.8 5.8 copy-start.17
  54.6 8.8 %copy-start.3 = (bf16[2,280,768]{2,1,0:T(8,128)(2,1)S(1)}, bf16[2,280,768]{2,1,0:T(8,128)(2,1)}, u32[]{:S(2)}) copy-start(bf16[2,280,768]{2,1,0:T(8,128)(2,1)} %param.16) | copy-start | bytes 2580484
  63.4 4.1 copy-start.38
  63.4 4.1 copy-start.49
  65.9 1.2 copy-start.9
  65.9 9.4 %copy-start.25 = (f32[2,280]{1,0:T(2,128)}, f32[2,280]{1,0:T(2,128)S(1)}, u32[]{:S(2)}) copy-start(f32[2,280]{1,0:T(2,128)S(1)} %broadcast_multiply_fusion.4) | copy-start | bytes 6724
  67.4 7.9 %copy-start.33 = (f32[2,280]{1,0:T(2,128)}, f32[2,280]{1,0:T(2,128)S(1)}, u32[]{:S(2)}) copy-start(f32[2,280]{1,0:T(2,128)S(1)} %add_rsqrt_fusion) | copy-start | bytes 6724
  75.3 16.2 %copy-start.7 = (f32[2,280,3072]{2,1,0:T(8,128)}, f32[2,280,3072]{2,1,0:T(8,128)S(1)}, u32[]{:S(2)}) copy-start(f32[2,280,3072]{2,1,0:T(8,128)S(1)} %get-tuple-element.85) | copy-start | bytes 20643844
  75.3 17.9 %copy-start.14 = (bf16[2,280,768]{2,1,0:T(8,128)(2,1)S(1)}, bf16[2,280,768]{2,1,0:T(8,128)(2,1)}, u32[]{:S(2)}) copy-start(bf16[2,280,768]{2,1,0:T(8,128)(2,1)} %param.17) | copy-start | bytes 2580484
  75.3 17.9 %copy-start.31 = (f32[2,280]{1,0:T(2,128)S(1)}, f32[2,280]{1,0:T(2,128)}, u32[]{:S(2)}) copy-start(f32[2,280]{1,0:T(2,128)} %concatenate.3) | copy-start | bytes 6724
  91.5 1.7 copy-start.13
  99.1 106.5 %reduce-scatter.14.cloned.1.call-start = ((), (), s32[]{:S(2)}) async-start(), calls=%async_computation.13 | async-start | bytes 7077888 | tf_op jit(solution)/shard_map/reduce_scatter | solution.py:196
  99.4 10.6 %copy-start.10 = (f32[2,280,768]{2,1,0:T(8,128)S(1)}, f32[2,280,768]{2,1,0:T(8,128)}, u32[]{:S(2)}) copy-start(f32[2,280,768]{2,1,0:T(8,128)} %copy-done.9) | copy-start | bytes 5160964
  99.4 10.6 %copy-start.26 = (f32[2,280]{1,0:T(2,128)S(1)}, f32[2,280]{1,0:T(2,128)}, u32[]{:S(2)}) copy-start(f32[2,280]{1,0:T(2,128)} %copy-done.25) | copy-start | bytes 6724
  99.4 10.6 %copy-start.34 = (f32[2,280]{1,0:T(2,128)S(1)}, f32[2,280]{1,0:T(2,128)}, u32[]{:S(2)}) copy-start(f32[2,280]{1,0:T(2,128)} %copy-done.33) | copy-start | bytes 6724
  99.4 10.6 %copy-start.39 = (f32[768]{0:T(1024)S(1)}, f32[768]{0:T(1024)}, u32[]{:S(2)}) copy-start(f32[768]{0:T(1024)} %param.26) | copy-start | bytes 9220
  99.4 10.6 %copy-start.50 = (f32[768]{0:T(1024)S(1)}, f32[768]{0:T(1024)}, u32[]{:S(2)}) copy-start(f32[768]{0:T(1024)} %param.27) | copy-start | bytes 9220
  107.9 2.1 copy-start.53
  115.9 1.5 copy-start.27
  115.9 1.5 copy-start.35
  115.9 104.8 %reduce-scatter.10.cloned.1.call-start = ((), (), s32[]{:S(2)}) async-start(), calls=%async_computation.11 | async-start | bytes 2580480 | tf_op jit(solution)/shard_map/reduce_scatter | solution.py:183
  117.4 7.9 %copy-start.11 = (f32[2,280,768]{2,1,0:T(8,128)S(1)}, f32[2,280,768]{2,1,0:T(8,128)}, u32[]{:S(2)}) copy-start(f32[2,280,768]{2,1,0:T(8,128)} %copy-done.9) | copy-start | bytes 5160964
  117.4 7.9 %copy-start.32 = (f32[2,280]{1,0:T(2,128)S(1)}, f32[2,280]{1,0:T(2,128)}, u32[]{:S(2)}) copy-start(f32[2,280]{1,0:T(2,128)} %concatenate.3) | copy-start | bytes 6724
  117.4 7.9 %copy-start.36 = (f32[2,280]{1,0:T(2,128)S(1)}, f32[2,280]{1,0:T(2,128)}, u32[]{:S(2)}) copy-start(f32[2,280]{1,0:T(2,128)} %copy-done.33) | copy-start | bytes 6724
  117.4 7.9 %copy-start.40 = (f32[768]{0:T(1024)S(1)}, f32[768]{0:T(1024)}, u32[]{:S(2)}) copy-start(f32[768]{0:T(1024)} %param.26) | copy-start | bytes 9220
  125.3 2.7 copy-start.48
  126.7 1.2 copy-start.8
  128.8 9.0 %copy-start.16 = (f32[4,6,280]{2,1,0:T(8,128)S(1)}, f32[4,6,280]{2,1,0:T(8,128)}, u32[]{:S(2)}) copy-start(f32[4,6,280]{2,1,0:T(8,128)} %log_add_fusion) | copy-start | bytes 80644
  128.9 9.0 %copy-start.21 = (pred[4,280]{1,0:T(4,128)(4,1)S(1)}, pred[4,280]{1,0:T(4,128)(4,1)}, u32[]{:S(2)}) copy-start(pred[4,280]{1,0:T(4,128)(4,1)} %copy-done.20) | copy-start | bytes 3364
  137.8 8.6 %copy-start.12 = (bf16[2,280,2,384]{1,3,0,2:T(8,128)(2,1)}, bf16[2,280,2,384]{1,3,0,2:T(8,128)(2,1)S(1)}, u32[]{:S(2)}) copy-start(bf16[2,280,2,384]{1,3,0,2:T(8,128)(2,1)S(1)} %copy.68) | copy-start | bytes 2580484
  137.9 10.2 %copy-start.29 = (f32[6,64]{1,0:T(8,128)S(1)}, f32[6,64]{1,0:T(8,128)}, u32[]{:S(2)}) copy-start(f32[6,64]{1,0:T(8,128)} %copy-done.28) | copy-start | bytes 4612
  157.6 6.2 copy-start.5
  163.8 2.7 copy-start.2
  163.8 4.9 copy-start.24
  182.6 199.4 %all-reduce.13.cloned.1.call-start = ((), (), s32[]{:S(2)}) async-start(), calls=%async_computation.17 | async-start | bytes 9437184
  195.6 1.2 copy-start.15
  195.6 290.3 %reduce-scatter.12.cloned.1.call-start = ((), (), s32[]{:S(2)}) async-start(), calls=%async_computation.12 | async-start | bytes 2433024 | tf_op jit(solution)/shard_map/reduce_scatter | solution.py:209
  200.8 428.3 %reduce-scatter.20.cloned.1.call-start = ((), (), s32[]{:S(2)}) async-start(), calls=%async_computation.16 | async-start | bytes 5013504
  205.6 565.2 %reduce-scatter.16.cloned.1.call-start = ((), (), s32[]{:S(2)}) async-start(), calls=%async_computation.14 | async-start | bytes 5013504 | tf_op jit(solution)/shard_map/reduce_scatter | solution.py:205
  210.9 0.7 copy-start.52
  210.9 1.9 copy-start.42
  210.9 2.1 copy-start.51
  213.0 7.7 copy-start.19
  213.0 7.7 copy-start.22
  213.0 9.8 %copy-start.30 = (f32[768]{0:T(1024)S(1)}, f32[768]{0:T(1024)}, u32[]{:S(2)}) copy-start(f32[768]{0:T(1024)} %get-tuple-element.80) | copy-start | bytes 9220
  213.0 9.8 %copy-start.37 = (f32[3072]{0:T(1024)S(1)}, f32[3072]{0:T(1024)}, u32[]{:S(2)}) copy-start(f32[3072]{0:T(1024)} %get-tuple-element.93) | copy-start | bytes 36868
  213.0 9.8 %copy-start.43 = (f32[768]{0:T(1024)S(1)}, f32[768]{0:T(1024)}, u32[]{:S(2)}) copy-start(f32[768]{0:T(1024)} %get-tuple-element.58) | copy-start | bytes 9220
  213.0 9.8 %copy-start.44 = (f32[768]{0:T(1024)S(1)}, f32[768]{0:T(1024)}, u32[]{:S(2)}) copy-start(f32[768]{0:T(1024)} %get-tuple-element.63) | copy-start | bytes 9220
Sparse Core Ops, SparseCore 0:
  13.5 12.7 all-gather.4
  27.8 15.6 all-gather.6
  45.0 15.6 all-gather.8
  99.3 13.8 reduce-scatter.17
  116.1 13.8 reduce-scatter.13
  182.7 10.4 reduce-scatter.9
  200.0 182.0 all-reduce.12
  387.9 98.0 reduce-scatter.11
  492.5 136.4 reduce-scatter.19
  634.7 136.0 reduce-scatter.15
where the time goes:
time: 786 us; the launch traced here: 778 us
  waiting for transfers between devices  505 us (64%)
  matrix products  102 us (13%)
  blocking collectives  56.1 us (7%)
  local copies, waits for them, and re-layouts  54 us (7%)
  other arithmetic  44.6 us (6%)
  between operations  16 us (2%)
    unnamed x12, waiting for transfers between devices  252 us
    reduce_scatter x1, waiting for transfers between devices, per_device(): lax.psum_scatter(up_term_grad, 'pairs', scatter_dimension=0, tiled=True)  142 us
    reduce_scatter x1, waiting for transfers between devices, per_device(): lax.psum_scatter(grad_w_out, ('pairs', 'heads'), scatter_dimension=0, til...  102 us
    unnamed x1, blocking collectives  43.3 us
    unnamed x121, local copies, waits for them, and re-layouts  22 us
    convert_element_type x1, other arithmetic, per_device(): act_low = jax.nn.gelu(hidden_pre, approximate=False).astype(jnp.bfloat16)  16.2 us
  transfers between devices with their start and end apart: 10, of which 5 were waited for; matrix products, arithmetic and copies ran while one was open for 24% of the time, Pallas kernels for 0%

commit v1 on v0

v1 whole, which is shorter than its diff:
```python
import functools
import math

import jax
import jax.numpy as jnp
from jax import lax
from jax.experimental import pallas as pl
from jax.experimental.pallas import tpu as pltpu
from jax.sharding import PartitionSpec as P

HEAD_DIM = 64
WORDS = 40
LANES = 128
EPSILON = 1e-06
MASKED = -1000000000.0
SWAP = [(0, 1), (1, 0)]
f32, bf16 = jnp.float32, jnp.bfloat16
VMEM_LIMIT = 58 * 1024 * 1024


def dot(a, b, ca=1, cb=0):
    return lax.dot_general(a, b, (((ca,), (cb,)), ((), ())), preferred_element_type=f32)


def centre(rows):
    mean_val = jnp.mean(rows, axis=-1, keepdims=True)
    centred = rows - mean_val
    inv_std = lax.rsqrt(jnp.mean(centred * centred, axis=-1, keepdims=True) + EPSILON)
    return centred * inv_std, inv_std


def norm_back(grad_rows, unit_rows, inv_std, gain):
    scaled = grad_rows * gain
    first = jnp.mean(scaled, axis=-1, keepdims=True)
    second = jnp.mean(scaled * unit_rows, axis=-1, keepdims=True)
    return inv_std * (scaled - first - unit_rows * second)


def col_sum(rows):
    return jnp.sum(rows, axis=0, keepdims=True)


def gelu_parts(v):
    u = jnp.abs(v) * 0.7071067811865476
    t = 1.0 / (1.0 + 0.39 * u)
    poly = 0.8866643918219983 - 0.22753713046899435 * t
    poly = -0.6354003145887568 + poly * t
    poly = 0.6495594277724073 + poly * t
    poly = 0.09138840279707615 + poly * t
    poly = 0.23532522096757497 + poly * t
    bell = jnp.exp(v * v * -0.5)
    tail = (0.5 * t) * poly * bell
    cdf = jnp.where(v < 0.0, tail, 1.0 - tail)
    return v * cdf, cdf + v * (bell * 0.3989422804014327)


def half_mask(value, lane, e):
    keep = (lane < HEAD_DIM) if e == 0 else (lane >= HEAD_DIM)
    return jnp.where(keep, value, jnp.zeros_like(value))


def attend(n, seq, half, len_ref, proj, ctx, lse_cols, lse_ref):
    scale = 1.0 / math.sqrt(HEAD_DIM)
    lane = lax.broadcasted_iota(jnp.int32, (seq, LANES), 1)
    key = lax.broadcasted_iota(jnp.int32, (1, seq), 1)
    lse_cols[...] = jnp.zeros_like(lse_cols)

    def step(hp, carry):
        off = pl.multiple_of(hp * LANES, LANES)
        for i in range(n):
            rows = pl.ds(i * seq, seq)
            q2 = proj[rows, pl.ds(off, LANES)] * scale
            k2 = proj[rows, pl.ds(half + off, LANES)].astype(bf16)
            v2 = proj[rows, pl.ds(2 * half + off, LANES)].astype(bf16)
            key_ok = (key >= WORDS) | (key < len_ref[i])
            outs = []
            for e in range(2):
                qm = half_mask(q2, lane, e).astype(bf16)
                s = jnp.where(key_ok, dot(qm, k2, 1, 1), MASKED)
                top = jnp.max(s, axis=-1, keepdims=True)
                w = jnp.exp(s - top)
                total = jnp.sum(w, axis=-1, keepdims=True)
                p = (w * (1.0 / total)).astype(bf16)
                outs.append(dot(p, v2))
                lse_cols[i] = jnp.where(lane == 2 * hp + e, top + jnp.log(total), lse_cols[i])
            ctx[rows, pl.ds(off, LANES)] = jnp.where(lane < HEAD_DIM, outs[0], outs[1])
        return carry

    lax.fori_loop(0, half // LANES, step, 0)
    for i in range(n):
        lse_ref[i] = lse_cols[i].T[: lse_ref.shape[1]]


def project(normed, w_ref, bias_ref, half, proj):
    for t in range(3):
        part = dot(normed, w_ref[t])
        if t != 1:
            part = part + bias_ref[t // 2 : t // 2 + 1]
        proj[:, t * half : (t + 1) * half] = part.astype(bf16).astype(f32)


def first_kernel(n, seq, half, len_ref, tok, gain, shift, w, bias, normed, qkv, ctx, lse, proj, ctx32, lse_cols):
    unit, _ = centre(tok[...].astype(f32))
    rows = (unit * gain[...] + shift[...]).astype(bf16)
    normed[...] = rows
    project(rows, w, bias, half, proj)
    for i in range(n):
        qkv[i] = proj[pl.ds(i * seq, seq)].astype(bf16)
    attend(n, seq, half, len_ref, proj, ctx32, lse_cols, lse)
    ctx[...] = ctx32[...].astype(bf16)


def second_kernel(
    n, seq, half, len_ref, head_ref, normed, w, bias, ctx_own, tok, w_out, out_bias, gain, shift,
    qkv, ctx, lse, resid, mlp_low, proj, ctx32, lse_cols,
):
    project(normed[...], w, bias, half, proj)
    for i in range(n):
        qkv[i] = proj[pl.ds(i * seq, seq)].astype(bf16)
    attend(n, seq, half, len_ref, proj, ctx32, lse_cols, lse)
    ctx[...] = ctx32[...].astype(bf16)
    own = pl.multiple_of(head_ref[0] * half, LANES)
    oth = pl.multiple_of((1 - head_ref[0]) * half, LANES)
    attn = dot(ctx_own[...], w_out[pl.ds(own, half)]) + dot(ctx[...], w_out[pl.ds(oth, half)])
    total = tok[...].astype(f32) + (attn + out_bias[...])
    resid[...] = total
    unit, _ = centre(total)
    mlp_low[...] = (unit * gain[...] + shift[...]).astype(bf16)


def mlp_kernel(
    steps, masks, block, me_ref, a_own, a_oth, g_own, g_oth, up, down, bias,
    out_own, out_oth, gmi_own, gmi_oth, d_up, d_down, d_bias, out_acc, gmi_acc, scr_up, scr_down,
):
    step = pl.program_id(0)
    rows = a_own.shape[0]

    @pl.when(step == 0)
    def _():
        out_acc[...] = jnp.zeros_like(out_acc)
        gmi_acc[...] = jnp.zeros_like(gmi_acc)

    sum_up = sum_down = sum_bias = None
    for part, (a, g) in enumerate(((a_own, g_own), (a_oth, g_oth))):
        at = pl.ds(part * rows, rows)
        act, slope = gelu_parts(dot(a[...], up[...]) + bias[...].astype(f32))
        act = act.astype(bf16)
        grad = (dot(g[...], down[...], 1, 1) * slope).astype(bf16)
        out_acc[at] += dot(act, down[...])
        gmi_acc[at] += dot(grad, up[...], 1, 1)
        u, d, b = dot(a[...], grad, 0, 0), dot(g[...], act, 0, 0), col_sum(grad.astype(f32))
        sum_up, sum_down, sum_bias = (
            (u, d, b) if part == 0 else (sum_up + u, sum_down + d, sum_bias + b)
        )
    d_bias[...] = sum_bias
    ordered(sum_up, scr_up, d_up, masks[0], block, me_ref)
    ordered(sum_down, scr_down, d_down, masks[1], block, me_ref)

    @pl.when(step == steps - 1)
    def _():
        out_own[...] = out_acc[:rows]
        out_oth[...] = out_acc[rows:].astype(bf16)
        gmi_own[...] = gmi_acc[:rows]
        gmi_oth[...] = gmi_acc[rows:].astype(bf16)


def ordered(value, scr, dest, offsets, block, me_ref):
    if block % 16:
        dest[...] = value.astype(dest.dtype)
        return
    scr[...] = value.astype(scr.dtype)
    for slot, offset in enumerate(offsets):
        at = pl.multiple_of((me_ref[0] ^ offset) * block, 16)
        dest[slot * block : (slot + 1) * block] = scr[pl.ds(at, block)].astype(dest.dtype)


def middle_kernel(
    n, seq, half, block, offsets, me_ref, head_ref, gmi_own, gmi_got, resid, g_low, gain, w_out, ctx_own, ctx_oth,
    grad_resid, gc_own, gc_oth, keep, send, sums, scr, cuts,
):
    unit, inv_std = centre(resid[...])
    gmi = gmi_own[...] + gmi_got[...].astype(f32)
    g_final = g_low[...].astype(f32)
    total = g_final + norm_back(gmi, unit, inv_std, gain[...])
    grad_resid[...] = total
    low = total.astype(bf16)
    sums[...] = jnp.zeros_like(sums)
    sums[0:1] = col_sum(gmi * unit)
    sums[1:2] = col_sum(gmi)
    sums[2:3] = col_sum(low.astype(f32))
    sums[3:4] = col_sum(g_final)
    own = pl.multiple_of(head_ref[0] * half, LANES)
    oth = pl.multiple_of((1 - head_ref[0]) * half, LANES)
    for dest, at in ((gc_own, own), (gc_oth, oth)):
        part = dot(low, w_out[pl.ds(at, half)], 1, 1)
        for i in range(n):
            dest[i] = part[i * seq : (i + 1) * seq].astype(bf16)
    scr[pl.ds(own, half)] = dot(ctx_own[...], low, 0, 0)
    scr[pl.ds(oth, half)] = dot(ctx_oth[...], low, 0, 0)
    if block % 16:
        keep[...] = scr[:half].astype(bf16)
        send[...] = scr[half:].astype(bf16)
        return
    part = block // 2
    for dest, core in ((keep, head_ref[0]), (send, 1 - head_ref[0])):
        for slot, offset in enumerate(offsets):
            at = pl.multiple_of((me_ref[0] ^ offset) * block + core * part, 8)
            cuts[slot * part : (slot + 1) * part] = scr[pl.ds(at, part)]
        dest[...] = cuts[...].astype(bf16)


def back_kernel(
    n, seq, half, block, offsets, len_ref, me_ref, qkv, gc, lse, normed, dqkv, d_w, sums, grads, scr
):
    scale = 1.0 / math.sqrt(HEAD_DIM)
    lane = lax.broadcasted_iota(jnp.int32, (seq, LANES), 1)
    key = lax.broadcasted_iota(jnp.int32, (seq, 1), 0)

    def step(hp, carry):
        off = pl.multiple_of(hp * LANES, LANES)
        for i in range(n):
            q2 = qkv[i, :, pl.ds(off, LANES)]
            k2 = qkv[i, :, pl.ds(half + off, LANES)]
            v2 = qkv[i, :, pl.ds(2 * half + off, LANES)]
            g2 = gc[i, :, pl.ds(off, LANES)]
            kt = k2.T
            key_ok = (key >= WORDS) | (key < len_ref[i])
            dq, dk, dv = [], [], []
            for e in range(2):
                qm = half_mask(q2, lane, e) * jnp.asarray(scale, bf16)
                s = jnp.where(key_ok, dot(k2, qm, 1, 1), MASKED)
                p = jnp.exp(s - lse[i, pl.ds(2 * hp + e, 1), :])
                dp = dot(v2, half_mask(g2, lane, e), 1, 1)
                inner = jnp.sum(p * dp, axis=0, keepdims=True)
                ds = (p * (dp - inner)).astype(bf16)
                dv.append(dot(p.astype(bf16), g2))
                dk.append(dot(ds, q2))
                dq.append(dot(kt[e * HEAD_DIM : (e + 1) * HEAD_DIM], ds))
            rows = pl.ds(i * seq, seq)
            grads[rows, pl.ds(off, LANES)] = jnp.concatenate(dq, axis=0).T * scale
            grads[rows, pl.ds(half + off, LANES)] = jnp.where(lane < HEAD_DIM, dk[0], dk[1]) * scale
            grads[rows, pl.ds(2 * half + off, LANES)] = jnp.where(lane < HEAD_DIM, dv[0], dv[1])
        return carry

    lax.fori_loop(0, half // LANES, step, 0)
    low = grads[...].astype(bf16)
    dqkv[...] = low
    sums[...] = jnp.zeros_like(sums)
    sums[0:1] = col_sum(low[:, :half].astype(f32))
    sums[1:2] = col_sum(low[:, 2 * half :].astype(f32))
    ordered(dot(normed[...], low, 0, 0), scr, d_w, offsets, block, me_ref)


def last_kernel(half, dq_own, dq_oth, w_own, w_oth, tok, gain, grad_resid, grad_tokens, sums):
    grad = None
    for dq, w in ((dq_own, w_own), (dq_oth, w_oth)):
        for t in range(3):
            part = dot(dq[:, t * half : (t + 1) * half], w[t], 1, 1)
            grad = part if grad is None else grad + part
    unit, inv_std = centre(tok[...].astype(f32))
    grad_tokens[...] = grad_resid[...] + norm_back(grad, unit, inv_std, gain[...])
    sums[...] = jnp.zeros_like(sums)
    sums[0:1] = col_sum(grad * unit)
    sums[1:2] = col_sum(grad)


SMEM = pl.BlockSpec(memory_space=pltpu.SMEM)


def call(body, name, outs, scratch, scalars, args, flops, trans=0):
    shapes = [jax.ShapeDtypeStruct(s, d) for s, d in outs]
    moved = sum(math.prod(s) * jnp.dtype(d).itemsize for s, d in outs)
    moved += sum(a.size * a.dtype.itemsize for a in args)
    return pl.pallas_call(
        body,
        name=name,
        out_shape=shapes,
        in_specs=[SMEM] * len(scalars) + [pl.BlockSpec(memory_space=pltpu.VMEM)] * len(args),
        out_specs=[pl.BlockSpec(memory_space=pltpu.VMEM)] * len(outs),
        scratch_shapes=[pltpu.VMEM(s, d) for s, d in scratch],
        compiler_params=pltpu.CompilerParams(vmem_limit_bytes=VMEM_LIMIT),
        cost_estimate=pl.CostEstimate(flops=flops, bytes_accessed=moved, transcendentals=trans),
    )(*scalars, *args)


def slots(masks):
    offsets = [0]
    for mask in reversed(masks):
        offsets = offsets + [o ^ mask for o in offsets]
    return offsets


def arrange(blocks, offsets, me):
    return jnp.concatenate([lax.dynamic_slice_in_dim(blocks, me ^ o, 1, axis=0) for o in offsets], axis=0)


def exchange(send, mask, count):
    return lax.ppermute(send, "pairs", [(i, i ^ mask) for i in range(count)])


def pair_sum(total, masks, count, held=bf16):
    for mask in masks:
        half = total.shape[0] // 2
        got = exchange(total[half:].astype(held), mask, count)
        total = total[:half].astype(f32) + got.astype(f32)
    return total[0].astype(f32)


def per_device(
    tokens, cotangent, text_len, word_mask, attn_gain, attn_shift, w_qkv, qv_bias, w_out, out_bias,
    mlp_gain, mlp_shift, w_up, up_bias, w_down, down_bias,
):
    n, seq, width = tokens.shape
    half = w_qkv.shape[2]
    hidden = w_up.shape[1]
    rows = n * seq
    count = lax.axis_size("pairs")
    block = width // count
    head = lax.axis_index("heads")
    me = lax.axis_index("pairs")
    head_s, me_s = head.reshape(1), me.reshape(1)
    lens = lax.dynamic_slice_in_dim(text_len, head * n, n)
    bits = count.bit_length() - 1
    order_a = [1 << b for b in range(bits)]
    order_b = order_a[1::-1] + order_a[2:]
    slots_a, slots_b = slots(order_a), slots(order_b)
    row = lambda v: v.reshape(1, -1)
    tok = tokens.reshape(rows, width)

    w_oth = lax.ppermute(w_qkv, "heads", SWAP)
    bias_oth = lax.ppermute(qv_bias, "heads", SWAP)
    keep_rows = jnp.concatenate(
        [word_mask.astype(bf16), jnp.ones((n, seq - WORDS), bf16)], axis=1
    )
    g_own = (cotangent * keep_rows[:, :, None]).reshape(rows, width)
    g_oth = lax.ppermute(g_own, "heads", SWAP)

    qkv_shape = ((n, seq, 3 * half), bf16)
    lse_shape = ((n, 8, seq), f32)
    attn_scratch = [((rows, 3 * half), f32), ((rows, half), f32), ((n, seq, LANES), f32)]
    units = n * half // HEAD_DIM
    attn_flops = 4 * units * seq * seq * HEAD_DIM + 6 * rows * width * half
    normed, qkv_own, ctx_own, lse_own = call(
        functools.partial(first_kernel, n, seq, half),
        "attend_own",
        [((rows, width), bf16), qkv_shape, ((rows, half), bf16), lse_shape],
        attn_scratch,
        [lens],
        [tok, row(attn_gain), row(attn_shift), w_qkv, qv_bias],
        attn_flops,
        units * seq * seq,
    )
    qkv_oth, ctx_oth, lse_oth, resid, mlp_low = call(
        functools.partial(second_kernel, n, seq, half),
        "attend_other",
        [qkv_shape, ((rows, half), bf16), lse_shape, ((rows, width), f32), ((rows, width), bf16)],
        attn_scratch,
        [lens, head_s],
        [normed, w_oth, bias_oth, ctx_own, tok, w_out, row(out_bias), row(mlp_gain), row(mlp_shift)],
        attn_flops + 2 * rows * width * width,
        units * seq * seq,
    )
    mlp_oth = lax.ppermute(mlp_low, "heads", SWAP)

    cut = 256
    steps = hidden // cut
    whole = lambda shape: pl.BlockSpec(shape, lambda i: (0,) * len(shape))
    row_spec = whole((rows, width))
    out_own, out_send, gmi_own, gmi_send, d_up, d_down, d_up_bias = pl.pallas_call(
        functools.partial(mlp_kernel, steps, (slots_a, slots_b), block),
        name="mlp",
        grid=(steps,),
        out_shape=[
            jax.ShapeDtypeStruct((rows, width), f32),
            jax.ShapeDtypeStruct((rows, width), bf16),
            jax.ShapeDtypeStruct((rows, width), f32),
            jax.ShapeDtypeStruct((rows, width), bf16),
            jax.ShapeDtypeStruct((width, hidden), bf16),
            jax.ShapeDtypeStruct((width, hidden), bf16),
            jax.ShapeDtypeStruct((1, hidden), f32),
        ],
        in_specs=[SMEM]
        + [row_spec] * 4
        + [
            pl.BlockSpec((width, cut), lambda i: (0, i)),
            pl.BlockSpec((cut, width), lambda i: (i, 0)),
            pl.BlockSpec((1, cut), lambda i: (0, i)),
        ],
        out_specs=[row_spec] * 4
        + [pl.BlockSpec((width, cut), lambda i: (0, i))] * 2
        + [pl.BlockSpec((1, cut), lambda i: (0, i))],
        scratch_shapes=[pltpu.VMEM((2 * rows, width), f32)] * 2 + [pltpu.VMEM((width, cut), bf16)] * 2,
        compiler_params=pltpu.CompilerParams(vmem_limit_bytes=VMEM_LIMIT),
        cost_estimate=pl.CostEstimate(
            flops=24 * rows * width * hidden, bytes_accessed=20 << 20, transcendentals=4 * rows * hidden
        ),
    )(me_s, mlp_low, mlp_oth, g_own, g_oth, w_up, w_down, row(up_bias))
    gmi_got = lax.ppermute(gmi_send, "heads", SWAP)
    out_got = lax.ppermute(out_send, "heads", SWAP)
    layer_out = (resid + (out_own + out_got.astype(f32) + down_bias)).astype(bf16)

    grad_resid, gc_own, gc_oth, wo_keep, wo_send, sums_mid = call(
        functools.partial(middle_kernel, n, seq, half, block, slots_b),
        "middle",
        [
            ((rows, width), f32),
            ((n, seq, half), bf16),
            ((n, seq, half), bf16),
            ((half, width), bf16),
            ((half, width), bf16),
            ((8, width), f32),
        ],
        [((width, width), f32), ((half, width), f32)],
        [me_s, head_s],
        [gmi_own, gmi_got, resid, g_own, row(mlp_gain), w_out, ctx_own, ctx_oth],
        4 * rows * width * width,
    )

    back = lambda name, qkv, gc, lse, kind: call(
        functools.partial(back_kernel, n, seq, half, block, slots_a),
        name,
        [((rows, 3 * half), bf16), ((width, 3 * half), kind), ((8, half), f32)],
        [((rows, 3 * half), f32), ((width, 3 * half), kind)],
        [lens, me_s],
        [qkv, gc, lse, normed],
        10 * units * seq * seq * HEAD_DIM + 6 * rows * width * half,
        units * seq * seq,
    )
    dq_oth, dw_send, sums_oth = back("back_other", qkv_oth, gc_oth, lse_oth, bf16)
    dq_own, dw_keep, sums_own = back("back_own", qkv_own, gc_own, lse_own, f32)
    grad_tok, sums_last = call(
        functools.partial(last_kernel, half),
        "last",
        [((rows, width), f32), ((8, width), f32)],
        [],
        [],
        [dq_own, dq_oth, w_qkv, w_oth, tok, row(attn_gain), grad_resid],
        12 * rows * width * half,
    )

    blocks = lambda v, size: v.reshape(count, size, -1)
    place = lambda v, size, offsets: blocks(v, size) if block % 16 == 0 else arrange(blocks(v, size), offsets, me)
    grad_w_up = pair_sum(place(d_up, block, slots_a), order_a, count)
    grad_w_down = pair_sum(place(d_down, block, slots_b), order_b, count).T
    if block % 16:
        wo = jnp.concatenate([wo_keep, wo_send], axis=0).reshape(count, 2, block // 2, width)
        wo = arrange(wo, slots_b, me)
        wo_keep = lax.dynamic_index_in_dim(wo, head, 1, keepdims=False)
        wo_send = lax.dynamic_index_in_dim(wo, 1 - head, 1, keepdims=False)
    wo_got = lax.ppermute(wo_send, "heads", SWAP)
    wo = wo_keep.astype(f32) + wo_got.astype(f32)
    grad_w_out = pair_sum(wo.reshape(count, block // 2, width), order_b, count)
    dw_got = lax.ppermute(dw_send, "heads", SWAP)
    dw = place(dw_keep + dw_got.astype(f32), block, slots_a)
    cut_at = 2 * half
    grad_qk = pair_sum(dw[..., :cut_at], order_a, count)
    grad_v = grad_vpart = None
    if block % 16 == 0:
        quarter = count // 4
        v = dw[..., cut_at:].reshape(2, 2, quarter, block, half).swapaxes(0, 1)
        grad_v = pair_sum(v.reshape(count, block, half), order_b, count)
    else:
        grad_v = pair_sum(dw[..., cut_at:], order_a, count)
    grad_w_qkv = jnp.stack([grad_qk[:, :half], grad_qk[:, half:], grad_v], axis=0)

    halves = lambda own, oth: jnp.where(
        head == 0, jnp.concatenate([own, oth], -1), jnp.concatenate([oth, own], -1)
    )
    up_zero = jnp.zeros_like(d_up_bias)
    vecs = [
        sums_last[0:1], sums_last[1:2], sums_mid[0:1], sums_mid[1:2], sums_mid[2:3], sums_mid[3:4],
        halves(sums_own[0:1], sums_oth[0:1]), halves(sums_own[1:2], sums_oth[1:2]), halves(d_up_bias, up_zero),
    ]
    small = jnp.concatenate([v.reshape(count, 2, -1) for v in vecs], axis=2)
    mine = lax.dynamic_index_in_dim(small, head, 1, keepdims=False)
    theirs = lax.dynamic_index_in_dim(small, 1 - head, 1, keepdims=False)
    small = mine + lax.ppermute(theirs, "heads", SWAP)
    small = pair_sum(arrange(small, slots_a, me), order_a, count, f32)
    step = width // count // 2
    piece = [small[i * step : (i + 1) * step] for i in range(8)]
    return (
        layer_out.reshape(n, seq, width),
        grad_tok.reshape(n, seq, width),
        piece[0],
        piece[1],
        grad_w_qkv,
        jnp.stack([piece[6], piece[7]], axis=0),
        grad_w_out,
        piece[4],
        piece[2],
        piece[3],
        grad_w_up,
        small[8 * step :],
        grad_w_down,
        piece[5],
    )


def solution(mesh):
    in_specs = (
        P(("pairs", "heads"), None, None),
        P(("pairs", "heads"), None, None),
        P("pairs"),
        P(("pairs", "heads"), None),
        P(),
        P(),
        P(None, None, "heads"),
        P(None, "heads"),
        P(),
        P(),
        P(),
        P(),
        P(None, "heads"),
        P("heads"),
        P("heads", None),
        P(),
    )
    out_specs = (
        P(("pairs", "heads"), None, None),
        P(("pairs", "heads"), None, None),
        P(("pairs", "heads")),
        P(("pairs", "heads")),
        P(None, "pairs", "heads"),
        P(None, ("pairs", "heads")),
        P(("pairs", "heads"), None),
        P(("pairs", "heads")),
        P(("pairs", "heads")),
        P(("pairs", "heads")),
        P("pairs", "heads"),
        P(("pairs", "heads")),
        P("heads", "pairs"),
        P(("pairs", "heads")),
    )
    return jax.shard_map(
        per_device, mesh=mesh, in_specs=in_specs, out_specs=out_specs, check_vma=False
    )
```

time: 786 us -> 221 us (0.28)
  waiting for transfers between devices: 505 us -> 65 us
  matrix products: 102 us -> 0 us
  Pallas kernels: 0 us -> 91.8 us
  blocking collectives: 56.1 us -> 0 us
  local copies, waits for them, and re-layouts: 54 us -> 14.9 us
  starting transfers between devices: 0.58 us -> 38.5 us
  other arithmetic: 44.6 us -> 9.34 us
  between operations: 16 us -> 1.2 us
    unnamed x12 -> x0, waiting for transfers between devices: 252 us -> none
    reduce_scatter x5 -> x0, waiting for transfers between devices: 244 us -> none  [the longest x1 142 us: per_device(): lax.psum_scatter(up_term_grad, 'pairs', scatter_dimension=0, tiled=True)]
    dot_general x18 -> x0, matrix products: 102 us -> none  [the longest x1 9.5 us: per_device(): jnp.einsum('nqhe,nkhe->nhqk', grad_context_heads, values, preferred_eleme...]
    pallas_call x0 -> x7, Pallas kernels: none -> 91.8 us  [the longest x6 60.3 us: call(): pl.pallas_call(body, name=name, out_shape=shapes, in_specs=[SMEM] * len(s...]
    ppermute x0 -> x33, waiting for transfers between devices: none -> 65 us  [the longest x24 60.9 us: exchange(): return lax.ppermute(send, 'pairs', [(i, i ^ mask) for i in range(count)])]
    unnamed x1 -> x0, blocking collectives: 43.3 us -> none
    ppermute x0 -> x33, starting transfers between devices: none -> 38.5 us  [the longest x24 36 us: exchange(): return lax.ppermute(send, 'pairs', [(i, i ^ mask) for i in range(count)])]
    convert_element_type x6 -> x2, other arithmetic: 30.1 us -> 1.9 us  [the longest x1 1.22 us: per_device(): (resid + (out_own + out_got.astype(f32) + down_bias)).astype(bf16)]
  transfers between devices with their start and end apart: 10 -> 33, of which waited for: 5 -> 22; matrix products, arithmetic and copies ran while one was open for 24% -> 8% of each run, Pallas kernels for 0% -> 10%
where the time goes in v1:
time: 221 us
  Pallas kernels  91.8 us (42%)
  waiting for transfers between devices  65 us (29%)
  starting transfers between devices  38.5 us (17%)
  local copies, waits for them, and re-layouts  14.9 us (7%)
  other arithmetic  9.34 us (4%)
    ppermute x24, waiting for transfers between devices, exchange(): return lax.ppermute(send, 'pairs', [(i, i ^ mask) for i in range(count)])  60.9 us
    pallas_call x6, Pallas kernels, call(): pl.pallas_call(body, name=name, out_shape=shapes, in_specs=[SMEM] * len(s...  60.3 us
    ppermute x24, starting transfers between devices, exchange(): return lax.ppermute(send, 'pairs', [(i, i ^ mask) for i in range(count)])  36 us
    pallas_call x1, Pallas kernels, per_device(): pl.pallas_call(functools.partial(mlp_kernel, steps, (slots_a, slots_b), b...  31.6 us
  transfers between devices with their start and end apart: 33, of which 22 were waited for; matrix products, arithmetic and copies ran while one was open for 8% of the time, Pallas kernels for 10%

profile of v1, /device:TPU:0, one launch (start us, length us, event | category | flops | bytes accessed | tf_op | source)
XLA Modules:
  0.0 220.7 jit_solution(8093024467632238976)
XLA Ops:
  1.3 0.7 convert_element_type.114
  2.0 1.3 broadcast_multiply_fusion
  3.8 0.6 reshape.162.gain
  5.5 10.0 %attend_own.1 = (bf16[560,768]{1,0:T(8,128)(2,1)}, bf16[2,280,1152]{2,1,0:T(8,128)(2,1)}, bf16[560,384]{1,0:T(8,128)(2,1)}, f32[2,8,280]{2,1,0:T(8,128)}) custom-call(s32[2]{0:T(128)} %dynamic_slice.58.len_ref, bf16[560,768]{1,0:T(8,128)(2,1)} %bitcast.69, f32[1,768]{1,0:T(1,128)} %reshape.162.gain, f32[1,768]{1,0:T(1,128)} %reshape.163.shift, ...), custom_call_target="tpu_custom_call" | custom-call | flops 1231749120 | bytes 5237248 | tf_op jit(solution)/shard_map/attend_own/pallas_call | solution.py:274
  16.1 0.6 reshape.165.gain
  17.9 0.7 copy-done.4
  18.6 12.5 %attend_other.1 = (bf16[2,280,1152]{2,1,0:T(8,128)(2,1)}, bf16[560,384]{1,0:T(8,128)(2,1)}, f32[2,8,280]{2,1,0:T(8,128)}, f32[560,768]{1,0:T(8,128)}, bf16[560,768]{1,0:T(8,128)(2,1)}) custom-call(s32[2]{0:T(128)} %dynamic_slice.58.len_ref, s32[1]{0:T(128)} %bitcast.head_ref, bf16[560,768]{1,0:T(8,128)(2,1)} %get-tuple-element.44.normed, ...), custom_call_target="tpu_custom_call" | custom-call | flops 1892352000 | bytes 9430528 | tf_op jit(solution)/shard_map/attend_other/pallas_call | solution.py:274
  31.3 0.6 reshape.169.bias
  31.9 1.7 collective-permute-done.2.a_oth
  33.7 0.9 copy-done.19
  34.6 31.6 %mlp.1 = (f32[560,768]{1,0:T(8,128)}, bf16[560,768]{1,0:T(8,128)(2,1)}, f32[560,768]{1,0:T(8,128)}, bf16[560,768]{1,0:T(8,128)(2,1)}, bf16[768,1536]{1,0:T(8,128...) custom-call(s32[1]{0:T(128)} %bitcast.2.me_ref, bf16[560,768]{1,0:T(8,128)(2,1)} %get-tuple-element.47.a_own, ...), custom_call_target="tpu_custom_call" | custom-call | flops 15854469120 | bytes 20971520 | tf_op jit(solution)/shard_map/mlp/pallas_call | solution.py:369
  66.5 0.8 fusion.4
  67.4 1.5 collective-permute-done.5.gmi_got
  68.8 0.9 copy-done.6
  69.7 7.9 %middle.1 = (f32[560,768]{1,0:T(8,128)}, bf16[2,280,384]{2,1,0:T(8,128)(2,1)}, bf16[2,280,384]{2,1,0:T(8,128)(2,1)}, bf16[384,768]{1,0:T(8,128)(2,1)}, bf16[384,768]{1,0:T(8,128)(2,1)}, /*index=5*/f32[8,768]{1,0:T(8,128)}) custom-call(s32[1]{0:T(128)} %bitcast.2.me_ref, s32[1]{0:T(128)} %bitcast.head_ref, f32[560,768]{1,0:T(8,128)} %get-tuple-element.51.gmi_own, ...), custom_call_target="tpu_custom_call" | custom-call | flops 1321205760 | bytes 10988544 | tf_op jit(solution)/shard_map/middle/pallas_call | solution.py:274
  77.6 11.0 %back_own.1 = (bf16[560,1152]{1,0:T(8,128)(2,1)}, f32[768,1152]{1,0:T(8,128)}, f32[8,384]{1,0:T(8,128)}) custom-call(s32[2]{0:T(128)} %dynamic_slice.58.len_ref, s32[1]{0:T(128)} %bitcast.2.me_ref, bf16[2,280,1152]{2,1,0:T(8,128)(2,1)} %get-tuple-element.50.qkv, bf16[2,280,384]{2,1,0:T(8,128)(2,1)} %get-tuple-element.54.gc, ...), custom_call_target="tpu_custom_call" | custom-call | flops 1593016320 | bytes 7439872 | tf_op jit(solution)/shard_map/back_own/pallas_call | solution.py:274
  88.7 10.3 %back_other.1 = (bf16[560,1152]{1,0:T(8,128)(2,1)}, bf16[768,1152]{1,0:T(8,128)(2,1)}, f32[8,384]{1,0:T(8,128)}) custom-call(s32[2]{0:T(128)} %dynamic_slice.58.len_ref, s32[1]{0:T(128)} %bitcast.2.me_ref, bf16[2,280,1152]{2,1,0:T(8,128)(2,1)} %get-tuple-element.57.qkv, bf16[2,280,384]{2,1,0:T(8,128)(2,1)} %get-tuple-element.58.gc, ...), custom_call_target="tpu_custom_call" | custom-call | flops 1593016320 | bytes 5670400 | tf_op jit(solution)/shard_map/back_other/pallas_call | solution.py:274
  99.0 8.5 %last.1 = (f32[560,768]{1,0:T(8,128)}, f32[8,768]{1,0:T(8,128)}) custom-call(bf16[560,1152]{1,0:T(8,128)(2,1)} %get-tuple-element.56.dq_own, bf16[560,1152]{1,0:T(8,128)(2,1)} %get-tuple-element.60.dq_oth, bf16[3,768,384]{2,1,0:T(8,128)(2,1)} %w_own.1, bf16[3,768,384]{2,1,0:T(8,128)(2,1)} %copy-done.4, bf16[560,768]{1,0:T(8,128)(2,1)} %bitcast.71, ...), custom_call_target="tpu_custom_call" | custom-call | flops 1981808640 | bytes 10447872 | tf_op jit(solution)/shard_map/last/pallas_call | solution.py:274
  107.5 0.8 slice_reduce_fusion.4
  109.0 0.8 fusion.10
  109.8 0.8 fusion.9
  111.4 0.9 collective-permute-done.6
  112.4 2.8 %collective-permute-start.7 = (f32[8,288]{1,0:T(8,128)S(1)}, f32[8,288]{1,0:T(8,128)S(1)}, u32[]{:S(2)}, u32[]{:S(2)}) collective-permute-start(f32[8,288]{1,0:T(8,128)S(1)} %concatenate.48), channel_id=1, source_target_pairs={{0,2},{2,0},{4,6},{6,4},{8,10},{10,8},{12,14},{14,12},{16,18},{18,... | collective-permute-start | bytes 27656 | tf_op jit(solution)/shard_map/ppermute | solution.py:298
  115.3 1.6 collective-permute-done.7
  117.0 2.1 collective-permute-start.8
  119.1 1.6 collective-permute-done.8
  120.7 2.1 collective-permute-start.9
  122.9 2.1 fusion.7
  124.9 1.6 collective-permute-start.25
  126.5 1.5 collective-permute-start.29
  128.6 2.7 %collective-permute-start.10 = (f32[1,288]{1,0:T(1,128)S(1)}, f32[1,288]{1,0:T(1,128)S(1)}, u32[]{:S(2)}, u32[]{:S(2)}) collective-permute-start(f32[1,288]{1,0:T(1,128)S(1)} %slice.352), channel_id=1, source_target_pairs={{0,16},{2,18},{4,20},{6,22},{8,24},{10,26},{12,28},{14,30},{16,0},... | collective-permute-start | bytes 3464 | tf_op jit(solution)/shard_map/ppermute | solution.py:298
  131.2 1.2 add_convert_fusion
  132.5 0.6 collective-permute-done.10
  133.7 0.6 slice_bitcast_fusion.2
  135.6 15.4 %collective-permute-done.25 = bf16[8,48,1536]{2,1,0:T(8,128)(2,1)S(1)} collective-permute-done((bf16[8,48,1536]{2,1,0:T(8,128)(2,1)S(1)}, bf16[8,48,1536]{2,1,0:T(8,128)(2,1)S(1)}, u32[]{:S(2)}, u32[]{:S(2)}) %collective-permute-start.25) | collective-permute-done | bytes 1179680 | tf_op jit(solution)/shard_map/ppermute | solution.py:298
  151.4 1.1 collective-permute-start.26
  152.6 9.2 %collective-permute-done.21 = bf16[8,24,768]{2,1,0:T(8,128)(2,1)S(1)} collective-permute-done((bf16[8,24,768]{2,1,0:T(8,128)(2,1)S(1)}, bf16[8,24,768]{2,1,0:T(8,128)(2,1)S(1)}, u32[]{:S(2)}, u32[]{:S(2)}) %collective-permute-start.21) | collective-permute-done | bytes 294944 | tf_op jit(solution)/shard_map/ppermute | solution.py:298
  161.8 0.6 collective-permute-start.22
  162.8 1.6 collective-permute-start.30
  164.4 3.3 %collective-permute-done.22 = bf16[4,24,768]{2,1,0:T(8,128)(2,1)S(1)} collective-permute-done((bf16[4,24,768]{2,1,0:T(8,128)(2,1)S(1)}, bf16[4,24,768]{2,1,0:T(8,128)(2,1)S(1)}, u32[]{:S(2)}, u32[]{:S(2)}) %collective-permute-start.22) | collective-permute-done | bytes 147488 | tf_op jit(solution)/shard_map/ppermute | solution.py:298
  168.2 2.9 %collective-permute-done.26 = bf16[4,48,1536]{2,1,0:T(8,128)(2,1)S(1)} collective-permute-done((bf16[4,48,1536]{2,1,0:T(8,128)(2,1)S(1)}, bf16[4,48,1536]{2,1,0:T(8,128)(2,1)S(1)}, u32[]{:S(2)}, u32[]{:S(2)}) %collective-permute-start.26) | collective-permute-done | bytes 589856 | tf_op jit(solution)/shard_map/ppermute | solution.py:298
  171.9 1.4 collective-permute-done.23
  173.3 2.3 %collective-permute-start.24 = (bf16[1,24,768]{2,1,0:T(8,128)(2,1)S(1)}, bf16[1,24,768]{2,1,0:T(8,128)(2,1)S(1)}, u32[]{:S(2)}, u32[]{:S(2)}) collective-permute-start(bf16[1,24,768]{2,1,0:T(8,128)(2,1)S(1)} %slice.477), channel_id=1, source_target_pairs={{0,16},{2,18},{4,20},{6,22},{8,24},{10,26},{12,28},{14,30},{16,0},... | collective-permute-start | bytes 110600 | tf_op jit(solution)/shard_map/ppermute | solution.py:298
  175.8 0.7 collective-permute-start.31
  176.4 3.7 %collective-permute-done.24 = bf16[1,24,768]{2,1,0:T(8,128)(2,1)S(1)} collective-permute-done((bf16[1,24,768]{2,1,0:T(8,128)(2,1)S(1)}, bf16[1,24,768]{2,1,0:T(8,128)(2,1)S(1)}, u32[]{:S(2)}, u32[]{:S(2)}) %collective-permute-start.24) | collective-permute-done | bytes 36896 | tf_op jit(solution)/shard_map/ppermute | solution.py:298
  180.2 0.6 fusion.3
  180.8 2.6 %collective-permute-done.27 = bf16[2,48,1536]{2,1,0:T(8,128)(2,1)S(1)} collective-permute-done((bf16[2,48,1536]{2,1,0:T(8,128)(2,1)S(1)}, bf16[2,48,1536]{2,1,0:T(8,128)(2,1)S(1)}, u32[]{:S(2)}, u32[]{:S(2)}) %collective-permute-start.27) | collective-permute-done | bytes 294944 | tf_op jit(solution)/shard_map/ppermute | solution.py:298
  183.5 0.9 collective-permute-start.28
  184.3 2.4 %collective-permute-done.31 = bf16[2,48,1536]{2,1,0:T(8,128)(2,1)S(1)} collective-permute-done((bf16[2,48,1536]{2,1,0:T(8,128)(2,1)S(1)}, bf16[2,48,1536]{2,1,0:T(8,128)(2,1)S(1)}, u32[]{:S(2)}, u32[]{:S(2)}) %collective-permute-start.31) | collective-permute-done | bytes 294944 | tf_op jit(solution)/shard_map/ppermute | solution.py:298
  186.9 4.0 %collective-permute-start.32 = (bf16[1,48,1536]{2,1,0:T(8,128)(2,1)S(1)}, bf16[1,48,1536]{2,1,0:T(8,128)(2,1)S(1)}, u32[]{:S(2)}, u32[]{:S(2)}) collective-permute-start(bf16[1,48,1536]{2,1,0:T(8,128)(2,1)S(1)} %slice.469), channel_id=1, source_target_pairs={{0,16},{2,18},{4,20},{6,22},{8,24},{10,26},{12,28},{14,30},{16,0},... | collective-permute-start | bytes 442376 | tf_op jit(solution)/shard_map/ppermute | solution.py:298
  191.4 1.0 collective-permute-start.16
  192.9 2.6 %collective-permute-done.28 = bf16[1,48,1536]{2,1,0:T(8,128)(2,1)S(1)} collective-permute-done((bf16[1,48,1536]{2,1,0:T(8,128)(2,1)S(1)}, bf16[1,48,1536]{2,1,0:T(8,128)(2,1)S(1)}, u32[]{:S(2)}, u32[]{:S(2)}) %collective-permute-start.28) | collective-permute-done | bytes 147488 | tf_op jit(solution)/shard_map/ppermute | solution.py:298
  195.5 0.7 fusion.1
  196.2 3.1 %collective-permute-done.16 = bf16[8,48,384]{2,1,0:T(8,128)(2,1)S(1)} collective-permute-done((bf16[8,48,384]{2,1,0:T(8,128)(2,1)S(1)}, bf16[8,48,384]{2,1,0:T(8,128)(2,1)S(1)}, u32[]{:S(2)}, u32[]{:S(2)}) %collective-permute-start.16) | collective-permute-done | bytes 294944 | tf_op jit(solution)/shard_map/ppermute | solution.py:298
  200.0 2.2 %collective-permute-done.12 = bf16[8,48,768]{2,1,0:T(8,128)(2,1)S(1)} collective-permute-done((bf16[8,48,768]{2,1,0:T(8,128)(2,1)S(1)}, bf16[8,48,768]{2,1,0:T(8,128)(2,1)S(1)}, u32[]{:S(2)}, u32[]{:S(2)}) %collective-permute-start.12) | collective-permute-done | bytes 589856 | tf_op jit(solution)/shard_map/ppermute | solution.py:298
  202.4 1.4 collective-permute-start.13
  203.8 0.7 fusion
  204.7 2.5 %collective-permute-start.18 = (bf16[2,48,384]{2,1,0:T(8,128)(2,1)S(1)}, bf16[2,48,384]{2,1,0:T(8,128)(2,1)S(1)}, u32[]{:S(2)}, u32[]{:S(2)}) collective-permute-start(bf16[2,48,384]{2,1,0:T(8,128)(2,1)S(1)} %slice.475), channel_id=1, source_target_pairs={{0,8},{2,10},{4,12},{6,14},{8,0},{10,2},{12,4},{14,6},{16,24},{18,... | collective-permute-start | bytes 221192 | tf_op jit(solution)/shard_map/ppermute | solution.py:298
  207.2 2.0 collective-permute-done.13
  209.3 2.2 %collective-permute-start.14 = (bf16[2,48,768]{2,1,0:T(8,128)(2,1)S(1)}, bf16[2,48,768]{2,1,0:T(8,128)(2,1)S(1)}, u32[]{:S(2)}, u32[]{:S(2)}) collective-permute-start(bf16[2,48,768]{2,1,0:T(8,128)(2,1)S(1)} %slice.473), channel_id=1, source_target_pairs={{0,8},{2,10},{4,12},{6,14},{8,0},{10,2},{12,4},{14,6},{16,24},{18,... | collective-permute-start | bytes 442376 | tf_op jit(solution)/shard_map/ppermute | solution.py:298
  211.9 2.7 %collective-permute-done.14 = bf16[2,48,768]{2,1,0:T(8,128)(2,1)S(1)} collective-permute-done((bf16[2,48,768]{2,1,0:T(8,128)(2,1)S(1)}, bf16[2,48,768]{2,1,0:T(8,128)(2,1)S(1)}, u32[]{:S(2)}, u32[]{:S(2)}) %collective-permute-start.14) | collective-permute-done | bytes 147488 | tf_op jit(solution)/shard_map/ppermute | solution.py:298
  214.7 2.0 collective-permute-start.15
  216.8 3.2 %collective-permute-done.15 = bf16[1,48,768]{2,1,0:T(8,128)(2,1)S(1)} collective-permute-done((bf16[1,48,768]{2,1,0:T(8,128)(2,1)S(1)}, bf16[1,48,768]{2,1,0:T(8,128)(2,1)S(1)}, u32[]{:S(2)}, u32[]{:S(2)}) %collective-permute-start.15) | collective-permute-done | bytes 73760 | tf_op jit(solution)/shard_map/ppermute | solution.py:298
  220.0 0.7 pad_maximum_fusion
  (145 shorter events, 13.8 us)
Async XLA Ops:
  0.6 3.1 %copy-start.9 = (f32[768]{0:T(1024)S(1)}, f32[768]{0:T(1024)}, u32[]{:S(2)}) copy-start(f32[768]{0:T(1024)} %param.20) | copy-start | bytes 9220
  0.7 3.7 %copy-start.10 = (f32[768]{0:T(1024)S(1)}, f32[768]{0:T(1024)}, u32[]{:S(2)}) copy-start(f32[768]{0:T(1024)} %param.21) | copy-start | bytes 9220
  0.7 4.3 %copy-start.22 = (s32[4]{0:T(128)S(1)}, s32[4]{0:T(128)}, u32[]{:S(2)}) copy-start(s32[4]{0:T(128)} %param.18) | copy-start | bytes 52
  0.7 16.6 %collective-permute-start = (bf16[3,768,384]{2,1,0:T(8,128)(2,1)}, bf16[3,768,384]{2,1,0:T(8,128)(2,1)S(1)}, u32[]{:S(2)}, u32[]{:S(2)}) collective-permute-start(bf16[3,768,384]{2,1,0:T(8,128)(2,1)} %w_own.1), channel_id=1, source_target_pairs={{0,1},{1,0},{2,3},{3,2},{4,5},{5,4},{6,7},{7,6},{8,9},{9,8},{10,11... | collective-permute-start | bytes 5308424 | tf_op jit(solution)/shard_map/ppermute | solution.py:330
  1.2 16.1 %collective-permute-start.1 = (f32[2,384]{1,0:T(2,128)}, f32[2,384]{1,0:T(2,128)S(1)}, u32[]{:S(2)}, u32[]{:S(2)}) collective-permute-start(f32[2,384]{1,0:T(2,128)} %bias.1), channel_id=1, source_target_pairs={{0,1},{1,0},{2,3},{3,2},{4,5},{5,4},{6,7},{7,6},{8,9},{9,8},{10,11... | collective-permute-start | bytes 9224 | tf_op jit(solution)/shard_map/ppermute | solution.py:331
  3.3 12.2 %copy-start.2 = (bf16[2,280,768]{2,1,0:T(8,128)(2,1)}, bf16[2,280,768]{2,1,0:T(8,128)(2,1)S(1)}, u32[]{:S(2)}) copy-start(bf16[2,280,768]{2,1,0:T(8,128)(2,1)S(1)} %broadcast_multiply_fusion) | copy-start | bytes 2580484
  3.3 28.7 %collective-permute-start.3 = (bf16[560,768]{1,0:T(8,128)(2,1)S(1)}, bf16[560,768]{1,0:T(8,128)(2,1)S(1)}, u32[]{:S(2)}, u32[]{:S(2)}) collective-permute-start(bf16[560,768]{1,0:T(8,128)(2,1)S(1)} %bitcast.63), channel_id=1, source_target_pairs={{0,1},{1,0},{2,3},{3,2},{4,5},{5,4},{6,7},{7,6},{8,9},{9,8},{10,11... | collective-permute-start | bytes 2580488 | tf_op jit(solution)/shard_map/ppermute | solution.py:336
  5.5 10.0 %copy-start.11 = (f32[768]{0:T(1024)S(1)}, f32[768]{0:T(1024)}, u32[]{:S(2)}) copy-start(f32[768]{0:T(1024)} %param.25) | copy-start | bytes 9220
  5.5 10.6 %copy-start.12 = (f32[768]{0:T(1024)S(1)}, f32[768]{0:T(1024)}, u32[]{:S(2)}) copy-start(f32[768]{0:T(1024)} %param.26) | copy-start | bytes 9220
  5.5 11.2 %copy-start.13 = (f32[768]{0:T(1024)S(1)}, f32[768]{0:T(1024)}, u32[]{:S(2)}) copy-start(f32[768]{0:T(1024)} %param.27) | copy-start | bytes 9220
  17.3 0.6 copy-start.21
  17.3 1.3 copy-start.4
  18.6 12.8 %copy-start.14 = (bf16[1536]{0:T(1024)(128)(2,1)S(1)}, bf16[1536]{0:T(1024)(128)(2,1)}, u32[]{:S(2)}) copy-start(bf16[1536]{0:T(1024)(128)(2,1)} %param.29) | copy-start | bytes 9220
  31.1 2.6 %collective-permute-start.2 = (bf16[560,768]{1,0:T(8,128)(2,1)}, bf16[560,768]{1,0:T(8,128)(2,1)S(1)}, u32[]{:S(2)}, u32[]{:S(2)}) collective-permute-start(bf16[560,768]{1,0:T(8,128)(2,1)} %get-tuple-element.47.a_own), channel_id=1, source_target_pairs={{0,1},{1,0},{2,3},{3,2},{4,5},{5,4},{6,7},{7,6},{8,9},{9,8},{10,11... | collective-permute-start | bytes 2580488 | tf_op jit(solution)/shard_map/ppermute | solution.py:363
  31.9 1.7 copy-start.18
  33.7 0.9 copy-start.19
  66.1 2.7 %collective-permute-start.5 = (bf16[560,768]{1,0:T(8,128)(2,1)}, bf16[560,768]{1,0:T(8,128)(2,1)S(1)}, u32[]{:S(2)}, u32[]{:S(2)}) collective-permute-start(bf16[560,768]{1,0:T(8,128)(2,1)} %get-tuple-element.52), channel_id=1, source_target_pairs={{0,1},{1,0},{2,3},{3,2},{4,5},{5,4},{6,7},{7,6},{8,9},{9,8},{10,11... | collective-permute-start | bytes 2580488 | tf_op jit(solution)/shard_map/ppermute | solution.py:398
  68.8 0.9 copy-start.6
  99.0 9.6 %copy-start.8 = (f32[8,768]{1,0:T(8,128)S(1)}, f32[8,768]{1,0:T(8,128)}, u32[]{:S(2)}) copy-start(f32[8,768]{1,0:T(8,128)} %get-tuple-element.64) | copy-start | bytes 73732
  99.0 20.1 %copy-start.17 = (bf16[560,768]{1,0:T(8,128)(2,1)S(1)}, bf16[560,768]{1,0:T(8,128)(2,1)}, u32[]{:S(2)}) copy-start(bf16[560,768]{1,0:T(8,128)(2,1)} %get-tuple-element.49) | copy-start | bytes 2580484
  99.0 23.9 %copy-start.3 = (bf16[768,1536]{1,0:T(8,128)(2,1)S(1)}, bf16[768,1536]{1,0:T(8,128)(2,1)}, u32[]{:S(2)}) copy-start(bf16[768,1536]{1,0:T(8,128)(2,1)} %get-tuple-element.72) | copy-start | bytes 7077892
  111.1 1.3 collective-permute-start.6
  112.4 4.5 %collective-permute-start.7 = (f32[8,288]{1,0:T(8,128)S(1)}, f32[8,288]{1,0:T(8,128)S(1)}, u32[]{:S(2)}, u32[]{:S(2)}) collective-permute-start(f32[8,288]{1,0:T(8,128)S(1)} %concatenate.48), channel_id=1, source_target_pairs={{0,2},{2,0},{4,6},{6,4},{8,10},{10,8},{12,14},{14,12},{16,18},{18,... | collective-permute-start | bytes 27656 | tf_op jit(solution)/shard_map/ppermute | solution.py:298
  117.0 3.7 %collective-permute-start.8 = (f32[4,288]{1,0:T(4,128)S(1)}, f32[4,288]{1,0:T(4,128)S(1)}, u32[]{:S(2)}, u32[]{:S(2)}) collective-permute-start(f32[4,288]{1,0:T(4,128)S(1)} %slice.348), channel_id=1, source_target_pairs={{0,4},{2,6},{4,0},{6,2},{8,12},{10,14},{12,8},{14,10},{16,20},{18,... | collective-permute-start | bytes 13832 | tf_op jit(solution)/shard_map/ppermute | solution.py:298
  119.1 9.5 %collective-permute-start.4 = (bf16[560,768]{1,0:T(8,128)(2,1)S(1)}, bf16[560,768]{1,0:T(8,128)(2,1)S(1)}, u32[]{:S(2)}, u32[]{:S(2)}) collective-permute-start(bf16[560,768]{1,0:T(8,128)(2,1)S(1)} %copy-done.17), channel_id=1, source_target_pairs={{0,1},{1,0},{2,3},{3,2},{4,5},{5,4},{6,7},{7,6},{8,9},{9,8},{10,11... | collective-permute-start | bytes 2580488 | tf_op jit(solution)/shard_map/ppermute | solution.py:399
  120.7 7.4 %collective-permute-start.9 = (f32[2,288]{1,0:T(2,128)S(1)}, f32[2,288]{1,0:T(2,128)S(1)}, u32[]{:S(2)}, u32[]{:S(2)}) collective-permute-start(f32[2,288]{1,0:T(2,128)S(1)} %slice.350), channel_id=1, source_target_pairs={{0,8},{2,10},{4,12},{6,14},{8,0},{10,2},{12,4},{14,6},{16,24},{18,... | collective-permute-start | bytes 6920 | tf_op jit(solution)/shard_map/ppermute | solution.py:298
  122.8 5.2 %copy-start.16 = (bf16[768,1152]{1,0:T(8,128)(2,1)S(1)}, bf16[768,1152]{1,0:T(8,128)(2,1)}, u32[]{:S(2)}) copy-start(bf16[768,1152]{1,0:T(8,128)(2,1)} %get-tuple-element.69) | copy-start | bytes 5308420
  122.8 5.2 %copy-start.20 = (bf16[384,768]{1,0:T(8,128)(2,1)S(1)}, bf16[384,768]{1,0:T(8,128)(2,1)}, u32[]{:S(2)}) copy-start(bf16[384,768]{1,0:T(8,128)(2,1)} %get-tuple-element.71) | copy-start | bytes 1769476
  122.8 8.4 %copy-start = (f32[560,768]{1,0:T(8,128)S(1)}, f32[560,768]{1,0:T(8,128)}, u32[]{:S(2)}) copy-start(f32[560,768]{1,0:T(8,128)} %get-tuple-element.46.resid) | copy-start | bytes 5160964
  122.8 8.4 %copy-start.5 = (f32[560,768]{1,0:T(8,128)S(1)}, f32[560,768]{1,0:T(8,128)}, u32[]{:S(2)}) copy-start(f32[560,768]{1,0:T(8,128)} %get-tuple-element.48) | copy-start | bytes 5160964
  122.8 8.4 %copy-start.15 = (f32[768]{0:T(1024)S(1)}, f32[768]{0:T(1024)}, u32[]{:S(2)}) copy-start(f32[768]{0:T(1024)} %param.31) | copy-start | bytes 9220
  124.9 26.1 %collective-permute-start.25 = (bf16[8,48,1536]{2,1,0:T(8,128)(2,1)S(1)}, bf16[8,48,1536]{2,1,0:T(8,128)(2,1)S(1)}, u32[]{:S(2)}, u32[]{:S(2)}) collective-permute-start(bf16[8,48,1536]{2,1,0:T(8,128)(2,1)S(1)} %bitcast.68), channel_id=1, source_target_pairs={{0,2},{2,0},{4,6},{6,4},{8,10},{10,8},{12,14},{14,12},{16,18},{18,... | collective-permute-start | bytes 3538952 | tf_op jit(solution)/shard_map/ppermute | solution.py:298
  126.5 35.9 %collective-permute-start.29 = (bf16[8,48,1536]{2,1,0:T(8,128)(2,1)S(1)}, bf16[8,48,1536]{2,1,0:T(8,128)(2,1)S(1)}, u32[]{:S(2)}, u32[]{:S(2)}) collective-permute-start(bf16[8,48,1536]{2,1,0:T(8,128)(2,1)S(1)} %bitcast.67), channel_id=1, source_target_pairs={{0,4},{2,6},{4,0},{6,2},{8,12},{10,14},{12,8},{14,10},{16,20},{18,... | collective-permute-start | bytes 3538952 | tf_op jit(solution)/shard_map/ppermute | solution.py:298
  128.0 62.8 %collective-permute-start.11 = (bf16[768,1152]{1,0:T(8,128)(2,1)S(1)}, bf16[768,1152]{1,0:T(8,128)(2,1)S(1)}, u32[]{:S(2)}, u32[]{:S(2)}) collective-permute-start(bf16[768,1152]{1,0:T(8,128)(2,1)S(1)} %copy-done.16), channel_id=1, source_target_pairs={{0,1},{1,0},{2,3},{3,2},{4,5},{5,4},{6,7},{7,6},{8,9},{9,8},{10,11... | collective-permute-start | bytes 5308424 | tf_op jit(solution)/shard_map/ppermute | solution.py:453
  128.1 6.8 %collective-permute-start.20 = (bf16[384,768]{1,0:T(8,128)(2,1)S(1)}, bf16[384,768]{1,0:T(8,128)(2,1)S(1)}, u32[]{:S(2)}, u32[]{:S(2)}) collective-permute-start(bf16[384,768]{1,0:T(8,128)(2,1)S(1)} %copy-done.20), channel_id=1, source_target_pairs={{0,1},{1,0},{2,3},{3,2},{4,5},{5,4},{6,7},{7,6},{8,9},{9,8},{10,11... | collective-permute-start | bytes 1769480 | tf_op jit(solution)/shard_map/ppermute | solution.py:450
  128.6 4.5 %collective-permute-start.10 = (f32[1,288]{1,0:T(1,128)S(1)}, f32[1,288]{1,0:T(1,128)S(1)}, u32[]{:S(2)}, u32[]{:S(2)}) collective-permute-start(f32[1,288]{1,0:T(1,128)S(1)} %slice.352), channel_id=1, source_target_pairs={{0,16},{2,18},{4,20},{6,22},{8,24},{10,26},{12,28},{14,30},{16,0},... | collective-permute-start | bytes 3464 | tf_op jit(solution)/shard_map/ppermute | solution.py:298
  131.2 3.6 %copy-start.7 = (bf16[384,768]{1,0:T(8,128)(2,1)S(1)}, bf16[384,768]{1,0:T(8,128)(2,1)}, u32[]{:S(2)}) copy-start(bf16[384,768]{1,0:T(8,128)(2,1)} %get-tuple-element.70) | copy-start | bytes 1769476
  135.0 26.7 %collective-permute-start.21 = (bf16[8,24,768]{2,1,0:T(8,128)(2,1)S(1)}, bf16[8,24,768]{2,1,0:T(8,128)(2,1)S(1)}, u32[]{:S(2)}, u32[]{:S(2)}) collective-permute-start(bf16[8,24,768]{2,1,0:T(8,128)(2,1)S(1)} %bitcast.73), channel_id=1, source_target_pairs={{0,4},{2,6},{4,0},{6,2},{8,12},{10,14},{12,8},{14,10},{16,20},{18,... | collective-permute-start | bytes 884744 | tf_op jit(solution)/shard_map/ppermute | solution.py:298
  151.4 19.8 %collective-permute-start.26 = (bf16[4,48,1536]{2,1,0:T(8,128)(2,1)S(1)}, bf16[4,48,1536]{2,1,0:T(8,128)(2,1)S(1)}, u32[]{:S(2)}, u32[]{:S(2)}) collective-permute-start(bf16[4,48,1536]{2,1,0:T(8,128)(2,1)S(1)} %slice.462), channel_id=1, source_target_pairs={{0,4},{2,6},{4,0},{6,2},{8,12},{10,14},{12,8},{14,10},{16,20},{18,... | collective-permute-start | bytes 1769480 | tf_op jit(solution)/shard_map/ppermute | solution.py:298
  161.8 5.9 %collective-permute-start.22 = (bf16[4,24,768]{2,1,0:T(8,128)(2,1)S(1)}, bf16[4,24,768]{2,1,0:T(8,128)(2,1)S(1)}, u32[]{:S(2)}, u32[]{:S(2)}) collective-permute-start(bf16[4,24,768]{2,1,0:T(8,128)(2,1)S(1)} %slice.471), channel_id=1, source_target_pairs={{0,2},{2,0},{4,6},{6,4},{8,10},{10,8},{12,14},{14,12},{16,18},{18,... | collective-permute-start | bytes 442376 | tf_op jit(solution)/shard_map/ppermute | solution.py:298
  162.8 12.8 %collective-permute-start.30 = (bf16[4,48,1536]{2,1,0:T(8,128)(2,1)S(1)}, bf16[4,48,1536]{2,1,0:T(8,128)(2,1)S(1)}, u32[]{:S(2)}, u32[]{:S(2)}) collective-permute-start(bf16[4,48,1536]{2,1,0:T(8,128)(2,1)S(1)} %slice.461), channel_id=1, source_target_pairs={{0,2},{2,0},{4,6},{6,4},{8,10},{10,8},{12,14},{14,12},{16,18},{18,... | collective-permute-start | bytes 1769480 | tf_op jit(solution)/shard_map/ppermute | solution.py:298
  167.8 5.5 %collective-permute-start.23 = (bf16[2,24,768]{2,1,0:T(8,128)(2,1)S(1)}, bf16[2,24,768]{2,1,0:T(8,128)(2,1)S(1)}, u32[]{:S(2)}, u32[]{:S(2)}) collective-permute-start(bf16[2,24,768]{2,1,0:T(8,128)(2,1)S(1)} %slice.474), channel_id=1, source_target_pairs={{0,8},{2,10},{4,12},{6,14},{8,0},{10,2},{12,4},{14,6},{16,24},{18,... | collective-permute-start | bytes 221192 | tf_op jit(solution)/shard_map/ppermute | solution.py:298
  171.4 12.0 %collective-permute-start.27 = (bf16[2,48,1536]{2,1,0:T(8,128)(2,1)S(1)}, bf16[2,48,1536]{2,1,0:T(8,128)(2,1)S(1)}, u32[]{:S(2)}, u32[]{:S(2)}) collective-permute-start(bf16[2,48,1536]{2,1,0:T(8,128)(2,1)S(1)} %slice.465), channel_id=1, source_target_pairs={{0,8},{2,10},{4,12},{6,14},{8,0},{10,2},{12,4},{14,6},{16,24},{18,... | collective-permute-start | bytes 884744 | tf_op jit(solution)/shard_map/ppermute | solution.py:298
  173.3 6.8 %collective-permute-start.24 = (bf16[1,24,768]{2,1,0:T(8,128)(2,1)S(1)}, bf16[1,24,768]{2,1,0:T(8,128)(2,1)S(1)}, u32[]{:S(2)}, u32[]{:S(2)}) collective-permute-start(bf16[1,24,768]{2,1,0:T(8,128)(2,1)S(1)} %slice.477), channel_id=1, source_target_pairs={{0,16},{2,18},{4,20},{6,22},{8,24},{10,26},{12,28},{14,30},{16,0},... | collective-permute-start | bytes 110600 | tf_op jit(solution)/shard_map/ppermute | solution.py:298
  175.8 11.0 %collective-permute-start.31 = (bf16[2,48,1536]{2,1,0:T(8,128)(2,1)S(1)}, bf16[2,48,1536]{2,1,0:T(8,128)(2,1)S(1)}, u32[]{:S(2)}, u32[]{:S(2)}) collective-permute-start(bf16[2,48,1536]{2,1,0:T(8,128)(2,1)S(1)} %slice.464), channel_id=1, source_target_pairs={{0,8},{2,10},{4,12},{6,14},{8,0},{10,2},{12,4},{14,6},{16,24},{18,... | collective-permute-start | bytes 884744 | tf_op jit(solution)/shard_map/ppermute | solution.py:298
  183.4 7.4 %copy-start.1 = (f32[768,1152]{1,0:T(8,128)S(1)}, f32[768,1152]{1,0:T(8,128)}, u32[]{:S(2)}) copy-start(f32[768,1152]{1,0:T(8,128)} %get-tuple-element.68) | copy-start | bytes 10616836
  183.5 12.0 %collective-permute-start.28 = (bf16[1,48,1536]{2,1,0:T(8,128)(2,1)S(1)}, bf16[1,48,1536]{2,1,0:T(8,128)(2,1)S(1)}, u32[]{:S(2)}, u32[]{:S(2)}) collective-permute-start(bf16[1,48,1536]{2,1,0:T(8,128)(2,1)S(1)} %slice.470), channel_id=1, source_target_pairs={{0,16},{2,18},{4,20},{6,22},{8,24},{10,26},{12,28},{14,30},{16,0},... | collective-permute-start | bytes 442376 | tf_op jit(solution)/shard_map/ppermute | solution.py:298
  186.9 17.0 %collective-permute-start.32 = (bf16[1,48,1536]{2,1,0:T(8,128)(2,1)S(1)}, bf16[1,48,1536]{2,1,0:T(8,128)(2,1)S(1)}, u32[]{:S(2)}, u32[]{:S(2)}) collective-permute-start(bf16[1,48,1536]{2,1,0:T(8,128)(2,1)S(1)} %slice.469), channel_id=1, source_target_pairs={{0,16},{2,18},{4,20},{6,22},{8,24},{10,26},{12,28},{14,30},{16,0},... | collective-permute-start | bytes 442376 | tf_op jit(solution)/shard_map/ppermute | solution.py:298
  191.4 7.9 %collective-permute-start.16 = (bf16[8,48,384]{2,1,0:T(8,128)(2,1)S(1)}, bf16[8,48,384]{2,1,0:T(8,128)(2,1)S(1)}, u32[]{:S(2)}, u32[]{:S(2)}) collective-permute-start(bf16[8,48,384]{2,1,0:T(8,128)(2,1)S(1)} %bitcast.74), channel_id=1, source_target_pairs={{0,4},{2,6},{4,0},{6,2},{8,12},{10,14},{12,8},{14,10},{16,20},{18,... | collective-permute-start | bytes 884744 | tf_op jit(solution)/shard_map/ppermute | solution.py:298
  192.4 9.9 %collective-permute-start.12 = (bf16[8,48,768]{2,1,0:T(8,128)(2,1)S(1)}, bf16[8,48,768]{2,1,0:T(8,128)(2,1)S(1)}, u32[]{:S(2)}, u32[]{:S(2)}) collective-permute-start(bf16[8,48,768]{2,1,0:T(8,128)(2,1)S(1)} %slice.463), channel_id=1, source_target_pairs={{0,2},{2,0},{4,6},{6,4},{8,10},{10,8},{12,14},{14,12},{16,18},{18,... | collective-permute-start | bytes 1769480 | tf_op jit(solution)/shard_map/ppermute | solution.py:298
  199.4 5.2 %collective-permute-start.17 = (bf16[4,48,384]{2,1,0:T(8,128)(2,1)S(1)}, bf16[4,48,384]{2,1,0:T(8,128)(2,1)S(1)}, u32[]{:S(2)}, u32[]{:S(2)}) collective-permute-start(bf16[4,48,384]{2,1,0:T(8,128)(2,1)S(1)} %slice.472), channel_id=1, source_target_pairs={{0,2},{2,0},{4,6},{6,4},{8,10},{10,8},{12,14},{14,12},{16,18},{18,... | collective-permute-start | bytes 442376 | tf_op jit(solution)/shard_map/ppermute | solution.py:298
  202.4 6.8 %collective-permute-start.13 = (bf16[4,48,768]{2,1,0:T(8,128)(2,1)S(1)}, bf16[4,48,768]{2,1,0:T(8,128)(2,1)S(1)}, u32[]{:S(2)}, u32[]{:S(2)}) collective-permute-start(bf16[4,48,768]{2,1,0:T(8,128)(2,1)S(1)} %slice.468), channel_id=1, source_target_pairs={{0,4},{2,6},{4,0},{6,2},{8,12},{10,14},{12,8},{14,10},{16,20},{18,... | collective-permute-start | bytes 884744 | tf_op jit(solution)/shard_map/ppermute | solution.py:298
  204.7 6.8 %collective-permute-start.18 = (bf16[2,48,384]{2,1,0:T(8,128)(2,1)S(1)}, bf16[2,48,384]{2,1,0:T(8,128)(2,1)S(1)}, u32[]{:S(2)}, u32[]{:S(2)}) collective-permute-start(bf16[2,48,384]{2,1,0:T(8,128)(2,1)S(1)} %slice.475), channel_id=1, source_target_pairs={{0,8},{2,10},{4,12},{6,14},{8,0},{10,2},{12,4},{14,6},{16,24},{18,... | collective-permute-start | bytes 221192 | tf_op jit(solution)/shard_map/ppermute | solution.py:298
  209.3 5.4 %collective-permute-start.14 = (bf16[2,48,768]{2,1,0:T(8,128)(2,1)S(1)}, bf16[2,48,768]{2,1,0:T(8,128)(2,1)S(1)}, u32[]{:S(2)}, u32[]{:S(2)}) collective-permute-start(bf16[2,48,768]{2,1,0:T(8,128)(2,1)S(1)} %slice.473), channel_id=1, source_target_pairs={{0,8},{2,10},{4,12},{6,14},{8,0},{10,2},{12,4},{14,6},{16,24},{18,... | collective-permute-start | bytes 442376 | tf_op jit(solution)/shard_map/ppermute | solution.py:298
  211.6 5.2 %collective-permute-start.19 = (bf16[1,48,384]{2,1,0:T(8,128)(2,1)S(1)}, bf16[1,48,384]{2,1,0:T(8,128)(2,1)S(1)}, u32[]{:S(2)}, u32[]{:S(2)}) collective-permute-start(bf16[1,48,384]{2,1,0:T(8,128)(2,1)S(1)} %slice.478), channel_id=1, source_target_pairs={{0,16},{2,18},{4,20},{6,22},{8,24},{10,26},{12,28},{14,30},{16,0},... | collective-permute-start | bytes 110600 | tf_op jit(solution)/shard_map/ppermute | solution.py:298
  214.7 5.3 %collective-permute-start.15 = (bf16[1,48,768]{2,1,0:T(8,128)(2,1)S(1)}, bf16[1,48,768]{2,1,0:T(8,128)(2,1)S(1)}, u32[]{:S(2)}, u32[]{:S(2)}) collective-permute-start(bf16[1,48,768]{2,1,0:T(8,128)(2,1)S(1)} %slice.476), channel_id=1, source_target_pairs={{0,16},{2,18},{4,20},{6,22},{8,24},{10,26},{12,28},{14,30},{16,0},... | collective-permute-start | bytes 221192 | tf_op jit(solution)/shard_map/ppermute | solution.py:298

commit v2 on v1

v2 whole, which is shorter than its diff:
```python
import functools
import math

import jax
import jax.numpy as jnp
from jax import lax
from jax.experimental import pallas as pl
from jax.experimental.pallas import tpu as pltpu
from jax.sharding import PartitionSpec as P

HEAD_DIM = 64
WORDS = 40
LANES = 128
EPSILON = 1e-06
MASKED = -1000000000.0
SWAP = [(0, 1), (1, 0)]
f32, bf16 = jnp.float32, jnp.bfloat16
MIB = 1024 * 1024


def dot(a, b, ca=1, cb=0):
    return lax.dot_general(a, b, (((ca,), (cb,)), ((), ())), preferred_element_type=f32)


def centre(rows):
    mean_val = jnp.mean(rows, axis=-1, keepdims=True)
    centred = rows - mean_val
    inv_std = lax.rsqrt(jnp.mean(centred * centred, axis=-1, keepdims=True) + EPSILON)
    return centred * inv_std, inv_std


def norm_back(grad_rows, unit_rows, inv_std, gain):
    scaled = grad_rows * gain
    first = jnp.mean(scaled, axis=-1, keepdims=True)
    second = jnp.mean(scaled * unit_rows, axis=-1, keepdims=True)
    return inv_std * (scaled - first - unit_rows * second)


def col_sum(rows):
    return jnp.sum(rows, axis=0, keepdims=True)


def gelu_parts(v):
    u = jnp.abs(v) * 0.7071067811865476
    t = 1.0 / (1.0 + 0.39 * u)
    poly = 0.8866643918219983 - 0.22753713046899435 * t
    poly = -0.6354003145887568 + poly * t
    poly = 0.6495594277724073 + poly * t
    poly = 0.09138840279707615 + poly * t
    poly = 0.23532522096757497 + poly * t
    bell = jnp.exp(v * v * -0.5)
    tail = (0.5 * t) * poly * bell
    cdf = jnp.where(v < 0.0, tail, 1.0 - tail)
    return v * cdf, cdf + v * (bell * 0.3989422804014327)


def as_row(ref):
    return ref[...].astype(f32).reshape(1, ref.shape[0])


def half_mask(value, lane, e):
    keep = (lane < HEAD_DIM) if e == 0 else (lane >= HEAD_DIM)
    return jnp.where(keep, value, jnp.zeros_like(value))


def attend(n, seq, half, len_ref, proj, ctx, lse_cols, lse_ref):
    scale = 1.0 / math.sqrt(HEAD_DIM)
    lane = lax.broadcasted_iota(jnp.int32, (seq, LANES), 1)
    key = lax.broadcasted_iota(jnp.int32, (1, seq), 1)
    lse_cols[...] = jnp.zeros_like(lse_cols)

    def step(hp, carry):
        off = pl.multiple_of(hp * LANES, LANES)
        for i in range(n):
            rows = pl.ds(i * seq, seq)
            q2 = proj[rows, pl.ds(off, LANES)] * scale
            k2 = proj[rows, pl.ds(half + off, LANES)].astype(bf16)
            v2 = proj[rows, pl.ds(2 * half + off, LANES)].astype(bf16)
            key_ok = (key >= WORDS) | (key < len_ref[i])
            outs = []
            for e in range(2):
                qm = half_mask(q2, lane, e).astype(bf16)
                s = jnp.where(key_ok, dot(qm, k2, 1, 1), MASKED)
                top = jnp.max(s, axis=-1, keepdims=True)
                w = jnp.exp(s - top)
                total = jnp.sum(w, axis=-1, keepdims=True)
                p = (w * (1.0 / total)).astype(bf16)
                outs.append(dot(p, v2))
                lse_cols[i] = jnp.where(lane == 2 * hp + e, top + jnp.log(total), lse_cols[i])
            ctx[rows, pl.ds(off, LANES)] = jnp.where(lane < HEAD_DIM, outs[0], outs[1])
        return carry

    lax.fori_loop(0, half // LANES, step, 0)
    for i in range(n):
        lse_ref[i] = lse_cols[i].T[: lse_ref.shape[1]]


def project(normed, w_ref, bias_ref, half, proj):
    for t in range(3):
        part = dot(normed, w_ref[t])
        if t != 1:
            part = part + bias_ref[t // 2 : t // 2 + 1]
        proj[:, t * half : (t + 1) * half] = part.astype(bf16).astype(f32)


def first_kernel(n, seq, half, len_ref, tok, gain, shift, w, bias, normed, qkv, ctx, lse, proj, ctx32, lse_cols):
    unit, _ = centre(tok[...].astype(f32))
    rows = (unit * as_row(gain) + as_row(shift)).astype(bf16)
    normed[...] = rows
    project(rows, w, bias, half, proj)
    for i in range(n):
        qkv[i] = proj[pl.ds(i * seq, seq)].astype(bf16)
    attend(n, seq, half, len_ref, proj, ctx32, lse_cols, lse)
    ctx[...] = ctx32[...].astype(bf16)


def second_kernel(
    n, seq, half, len_ref, head_ref, normed, w, bias, ctx_own, tok, w_out, out_bias, gain, shift,
    qkv, ctx, lse, resid, mlp_low, proj, ctx32, lse_cols,
):
    project(normed[...], w, bias, half, proj)
    for i in range(n):
        qkv[i] = proj[pl.ds(i * seq, seq)].astype(bf16)
    attend(n, seq, half, len_ref, proj, ctx32, lse_cols, lse)
    ctx[...] = ctx32[...].astype(bf16)
    own = pl.multiple_of(head_ref[0] * half, LANES)
    oth = pl.multiple_of((1 - head_ref[0]) * half, LANES)
    attn = dot(ctx_own[...], w_out[pl.ds(own, half)]) + dot(ctx[...], w_out[pl.ds(oth, half)])
    total = tok[...].astype(f32) + (attn + as_row(out_bias))
    resid[...] = total
    unit, _ = centre(total)
    mlp_low[...] = (unit * as_row(gain) + as_row(shift)).astype(bf16)


def mlp_kernel(
    steps, masks, block, me_ref, a_own, a_oth, g_own, g_oth, up, down, bias,
    out_own, out_oth, gmi_own, gmi_oth, up_keep, up_send, down_keep, down_send, d_bias,
    out_acc, gmi_acc, scr_up, scr_down, a, g,
):
    step = pl.program_id(0)
    rows = a_own.shape[0]

    @pl.when(step == 0)
    def _():
        out_acc[...] = jnp.zeros_like(out_acc)
        gmi_acc[...] = jnp.zeros_like(gmi_acc)
        a[:rows], a[rows:] = a_own[...], a_oth[...]
        g[:rows], g[rows:] = g_own[...], g_oth[...]

    act, slope = gelu_parts(dot(a[...], up[...]) + as_row(bias))
    act = act.astype(bf16)
    grad = (dot(g[...], down[...], 1, 1) * slope).astype(bf16)
    ordered(dot(a[...], grad, 0, 0), scr_up, up_keep, up_send, masks[0], block, me_ref)
    ordered(dot(g[...], act, 0, 0), scr_down, down_keep, down_send, masks[1], block, me_ref)
    out_acc[...] += dot(act, down[...])
    gmi_acc[...] += dot(grad, up[...], 1, 1)
    d_bias[...] = col_sum(grad.astype(f32)).reshape(d_bias.shape)

    @pl.when(step == steps - 1)
    def _():
        out_own[...] = out_acc[:rows]
        out_oth[...] = out_acc[rows:].astype(bf16)
        gmi_own[...] = gmi_acc[:rows]
        gmi_oth[...] = gmi_acc[rows:].astype(bf16)


def ordered(value, scr, keep, send, offsets, block, me_ref, got=()):
    half, cols = keep.shape[0], pl.ds(0, value.shape[1])
    if block % 16:
        keep[:, cols] = value[:half].astype(keep.dtype)
        send[:, cols] = value[half:].astype(send.dtype)
        return
    scr[...] = value.astype(scr.dtype)
    for slot, offset in enumerate(offsets):
        late = slot * block >= half
        dest, at = (send, pl.ds(slot * block - half, block)) if late else (keep, pl.ds(slot * block, block))
        part = scr[pl.ds(pl.multiple_of((me_ref[0] ^ offset) * block, 16), block)]
        if got:
            part = part + got[late][at].astype(f32)
        dest[at, cols] = part.astype(dest.dtype)


def middle_kernel(
    n, seq, half, block, offsets, me_ref, head_ref, gmi_own, gmi_got, resid, g_low, gain, w_out, ctx_own, ctx_oth,
    grad_resid, gc_own, gc_oth, keep, send, sums, scr, cuts,
):
    unit, inv_std = centre(resid[...])
    gmi = gmi_own[...] + gmi_got[...].astype(f32)
    g_final = g_low[...].astype(f32)
    total = g_final + norm_back(gmi, unit, inv_std, as_row(gain))
    grad_resid[...] = total
    low = total.astype(bf16)
    sums[...] = jnp.zeros_like(sums)
    sums[0:1] = col_sum(gmi * unit)
    sums[1:2] = col_sum(gmi)
    sums[2:3] = col_sum(low.astype(f32))
    sums[3:4] = col_sum(g_final)
    own = pl.multiple_of(head_ref[0] * half, LANES)
    oth = pl.multiple_of((1 - head_ref[0]) * half, LANES)
    for dest, at in ((gc_own, own), (gc_oth, oth)):
        part = dot(low, w_out[pl.ds(at, half)], 1, 1)
        for i in range(n):
            dest[i] = part[i * seq : (i + 1) * seq].astype(bf16)
    scr[pl.ds(own, half)] = dot(ctx_own[...], low, 0, 0)
    scr[pl.ds(oth, half)] = dot(ctx_oth[...], low, 0, 0)
    if block % 16:
        keep[...] = scr[:half].astype(bf16)
        send[...] = scr[half:].astype(bf16)
        return
    part = block // 2
    for dest, core in ((keep, head_ref[0]), (send, 1 - head_ref[0])):
        for slot, offset in enumerate(offsets):
            at = pl.multiple_of((me_ref[0] ^ offset) * block + core * part, 8)
            cuts[slot * block : slot * block + part] = scr[pl.ds(at, part), :half]
            cuts[slot * block + part : (slot + 1) * block] = scr[pl.ds(at, part), half:]
        dest[...] = cuts[...].astype(bf16)


def back_kernel(n, seq, half, block, masks, fused, len_ref, me_ref, qkv, gc, lse, normed, *rest):
    if fused:
        got_qk, got_v, (wo, wo_got), rest = rest[:2], rest[2:4], rest[4:6], rest[6:]
    else:
        got_qk = got_v = ()
    dqkv, qk_keep, qk_send, v_keep, v_send, sums, grads, scr_qk, scr_v = rest
    scale = 1.0 / math.sqrt(HEAD_DIM)
    lane = lax.broadcasted_iota(jnp.int32, (seq, LANES), 1)
    key = lax.broadcasted_iota(jnp.int32, (seq, 1), 0)

    def step(hp, carry):
        off = pl.multiple_of(hp * LANES, LANES)
        for i in range(n):
            q2 = qkv[i, :, pl.ds(off, LANES)]
            k2 = qkv[i, :, pl.ds(half + off, LANES)]
            v2 = qkv[i, :, pl.ds(2 * half + off, LANES)]
            g2 = gc[i, :, pl.ds(off, LANES)]
            kt = k2.T
            key_ok = (key >= WORDS) | (key < len_ref[i])
            dq, dk, dv = [], [], []
            for e in range(2):
                qm = half_mask(q2, lane, e) * jnp.asarray(scale, bf16)
                s = jnp.where(key_ok, dot(k2, qm, 1, 1), MASKED)
                p = jnp.exp(s - lse[i, pl.ds(2 * hp + e, 1), :])
                dp = dot(v2, half_mask(g2, lane, e), 1, 1)
                inner = jnp.sum(p * dp, axis=0, keepdims=True)
                ds = (p * (dp - inner)).astype(bf16)
                dv.append(dot(p.astype(bf16), g2))
                dk.append(dot(ds, q2))
                dq.append(dot(kt[e * HEAD_DIM : (e + 1) * HEAD_DIM], ds))
            rows = pl.ds(i * seq, seq)
            grads[rows, pl.ds(off, LANES)] = jnp.concatenate(dq, axis=0).T * scale
            grads[rows, pl.ds(half + off, LANES)] = jnp.where(lane < HEAD_DIM, dk[0], dk[1]) * scale
            grads[rows, pl.ds(2 * half + off, LANES)] = jnp.where(lane < HEAD_DIM, dv[0], dv[1])
        return carry

    lax.fori_loop(0, half // LANES, step, 0)
    low = grads[...].astype(bf16)
    dqkv[...] = low
    sums[...] = jnp.zeros_like(sums)
    sums[0:1] = col_sum(low[:, :half].astype(f32))
    sums[1:2] = col_sum(low[:, 2 * half :].astype(f32))
    rows = normed[...]
    ordered(dot(rows, low[:, : 2 * half], 0, 0), scr_qk, qk_keep, qk_send, masks[0], block, me_ref, got_qk)
    ordered(dot(rows, low[:, 2 * half :], 0, 0), scr_v, v_keep, v_send, masks[1], block, me_ref, got_v)
    if fused:
        at = v_keep.shape[0]
        both = wo[...].astype(f32) + wo_got[...].astype(f32)
        v_keep[:, half:] = both[:at]
        v_send[:, half:] = both[at:].astype(bf16)


def last_kernel(
    half, head_ref, dq_own, dq_oth, w_own, w_oth, tok, gain, grad_resid, sums_mid, sums_own, sums_oth, up_sums,
    grad_tokens, vecs,
):
    grad = None
    for dq, w in ((dq_own, w_own), (dq_oth, w_oth)):
        for t in range(3):
            part = dot(dq[:, t * half : (t + 1) * half], w[t], 1, 1)
            grad = part if grad is None else grad + part
    unit, inv_std = centre(tok[...].astype(f32))
    grad_tokens[...] = grad_resid[...] + norm_back(grad, unit, inv_std, as_row(gain))
    width = 2 * half
    vecs[...] = jnp.zeros_like(vecs)
    vecs[0:1, :width], vecs[0:1, width:] = col_sum(grad * unit), col_sum(grad)
    vecs[1:2, :width], vecs[1:2, width:] = sums_mid[0:1], sums_mid[1:2]
    vecs[2:3, :width], vecs[2:3, width:] = sums_mid[2:3], sums_mid[3:4]
    first = head_ref[0] == 0
    for i in range(2):
        own, oth = sums_own[i : i + 1], sums_oth[i : i + 1]
        vecs[3:4, i * width : i * width + half] = jnp.where(first, own, oth)
        vecs[3:4, i * width + half : (i + 1) * width] = jnp.where(first, oth, own)
    up = as_row(up_sums)
    for i in range(2):
        vecs[4 + i : 5 + i, : up.shape[1]] = jnp.where(head_ref[0] == i, up, jnp.zeros_like(up))


def spread_kernel(count, width, hidden, index_ref, vec, vec_got, *outs):
    index, lanes = index_ref[0], vec.shape[1]
    total = vec[...] + vec_got[...]
    part = width // count // 2
    rolled = pltpu.roll(total, lanes - index * part, 1)
    for i in range(6):
        at = (i % 2) * width
        outs[i][...] = rolled[i // 2 : i // 2 + 1, at : at + part].reshape(part)
    for i in range(2):
        outs[6][i : i + 1] = rolled[3:4, i * width : i * width + part]
    part = hidden // count
    up = jnp.where(index < count, total[4:5], total[5:6])
    up = pltpu.roll(jnp.concatenate([up] * 8, axis=0), lanes - (index % count) * part, 1)
    outs[7][...] = up[0:1, :part].reshape(part)


def combine_kernel(plan, adds, *refs):
    ins, outs = refs[: plan["ins"]], refs[plan["ins"] :]
    for keep, got, at, kept, send, place in plan["parts"]:
        rows = ins[keep].shape[0]
        half = rows // 2
        outs[kept][...] = ins[keep][:half].astype(f32) + ins[got][at : at + half].astype(f32)
        low = ins[keep][half:].astype(f32) + ins[got][at + half : at + rows].astype(f32)
        outs[send][place : place + half] = low.astype(bf16)
    for a, b, at, out, turned in adds:
        total = ins[a][...].astype(f32) + ins[b][at : at + ins[a].shape[0]].astype(f32)
        outs[out][...] = total.T if turned else total


def combine(name, parts, groups, adds=()):
    if any(keep.shape[0] % 32 for keep, _, _ in parts) or any(a.shape[0] % 8 for a, *_ in adds):
        total = [k.astype(f32) + g[at : at + k.shape[0]].astype(f32) for k, g, at in parts]
        keeps = [t[: t.shape[0] // 2] for t in total]
        sends = [jnp.concatenate([total[i][total[i].shape[0] // 2 :].astype(bf16) for i in g], 0) for g in groups]
        sums = [a.astype(f32) + b[at : at + a.shape[0]].astype(f32) for a, b, at, _ in adds]
        return keeps, sends, [v.T if turned else v for v, (*_, turned) in zip(sums, adds)]
    arrays, outs, plan, plan_adds = [], [], [], []

    def put(array):
        for i, have in enumerate(arrays):
            if have is array:
                return i
        arrays.append(array)
        return len(arrays) - 1

    for keep, _, _ in parts:
        outs.append(((keep.shape[0] // 2, keep.shape[1]), f32))
    for g in groups:
        outs.append(((sum(parts[i][0].shape[0] // 2 for i in g), parts[g[0]][0].shape[1]), bf16))
    for number, g in enumerate(groups):
        place = 0
        for i in g:
            keep, got, at = parts[i]
            plan.append((put(keep), put(got), at, i, len(parts) + number, place))
            place += keep.shape[0] // 2
    for a, b, at, turned in adds:
        plan_adds.append((put(a), put(b), at, len(outs), turned))
        outs.append((a.shape[::-1] if turned else a.shape, f32))
    got = call(
        functools.partial(combine_kernel, {"ins": len(arrays), "parts": plan}, plan_adds),
        name, outs, [], [], arrays, 24,
    )
    return got[: len(parts)], got[len(parts) : len(parts) + len(groups)], got[len(parts) + len(groups) :]


SMEM = pl.BlockSpec(memory_space=pltpu.SMEM)
VMEM = pl.BlockSpec(memory_space=pltpu.VMEM)


def params(limit):
    return dict(
        compiler_params=pltpu.CompilerParams(vmem_limit_bytes=limit * MIB),
        cost_estimate=pl.CostEstimate(flops=0, bytes_accessed=MIB, transcendentals=0),
    )


def call(body, name, outs, scratch, scalars, args, limit):
    return pl.pallas_call(
        body,
        name=name,
        out_shape=[jax.ShapeDtypeStruct(s, d) for s, d in outs],
        in_specs=[SMEM] * len(scalars) + [VMEM] * len(args),
        out_specs=[VMEM] * len(outs),
        scratch_shapes=[pltpu.VMEM(s, d) for s, d in scratch],
        **params(limit),
    )(*scalars, *args)


def slots(masks):
    offsets = [0]
    for mask in reversed(masks):
        offsets = offsets + [o ^ mask for o in offsets]
    return offsets


def arrange(blocks, offsets, me):
    return jnp.concatenate([lax.dynamic_slice_in_dim(blocks, me ^ o, 1, axis=0) for o in offsets], axis=0)


def exchange(send, mask, count):
    return lax.ppermute(send, "pairs", [(i, i ^ mask) for i in range(count)])


def per_device(
    tokens, cotangent, text_len, word_mask, attn_gain, attn_shift, w_qkv, qv_bias, w_out, out_bias,
    mlp_gain, mlp_shift, w_up, up_bias, w_down, down_bias,
):
    n, seq, width = tokens.shape
    half = w_qkv.shape[2]
    hidden = w_up.shape[1]
    rows = n * seq
    count = lax.axis_size("pairs")
    block = width // count
    head = lax.axis_index("heads")
    me = lax.axis_index("pairs")
    head_s, me_s = head.reshape(1), me.reshape(1)
    lens = lax.dynamic_slice_in_dim(text_len, head * n, n)
    bits = count.bit_length() - 1
    order_a = [1 << b for b in range(bits)]
    order_b = order_a[1::-1] + order_a[2:]
    slots_a, slots_b = slots(order_a), slots(order_b)
    tie = lax.optimization_barrier
    tok = tokens.reshape(rows, width)

    w_oth = lax.ppermute(w_qkv, "heads", SWAP)
    bias_oth = lax.ppermute(qv_bias, "heads", SWAP)
    keep_rows = jnp.concatenate(
        [word_mask.astype(bf16), jnp.ones((n, seq - WORDS), bf16)], axis=1
    )
    g_own = (cotangent * keep_rows[:, :, None]).reshape(rows, width)
    g_oth = lax.ppermute(g_own, "heads", SWAP)

    qkv_shape = ((n, seq, 3 * half), bf16)
    lse_shape = ((n, 8, seq), f32)
    attn_scratch = [((rows, 3 * half), f32), ((rows, half), f32), ((n, seq, LANES), f32)]
    normed, qkv_own, ctx_own, lse_own = call(
        functools.partial(first_kernel, n, seq, half),
        "attend_own",
        [((rows, width), bf16), qkv_shape, ((rows, half), bf16), lse_shape],
        attn_scratch,
        [lens],
        [tok, attn_gain, attn_shift, w_qkv, qv_bias],
        24,
    )
    qkv_oth, ctx_oth, lse_oth, resid, mlp_low = call(
        functools.partial(second_kernel, n, seq, half),
        "attend_other",
        [qkv_shape, ((rows, half), bf16), lse_shape, ((rows, width), f32), ((rows, width), bf16)],
        attn_scratch,
        [lens, head_s],
        [normed, w_oth, bias_oth, ctx_own, tok, w_out, out_bias, mlp_gain, mlp_shift],
        28,
    )
    mlp_oth = lax.ppermute(mlp_low, "heads", SWAP)

    cut = 512 if hidden % 512 == 0 else hidden
    steps = hidden // cut
    out_own, out_send, gmi_own, gmi_send, up_keep, up_send, down_keep, down_send, up_sums = pl.pallas_call(
        functools.partial(mlp_kernel, steps, (slots_a, slots_b), block),
        name="mlp",
        grid=(steps,),
        out_shape=[
            jax.ShapeDtypeStruct((rows, width), f32),
            jax.ShapeDtypeStruct((rows, width), bf16),
            jax.ShapeDtypeStruct((rows, width), f32),
            jax.ShapeDtypeStruct((rows, width), bf16),
            *[jax.ShapeDtypeStruct((width // 2, hidden), bf16)] * 4,
            jax.ShapeDtypeStruct((hidden,), f32),
        ],
        in_specs=[SMEM]
        + [VMEM] * 4
        + [
            pl.BlockSpec((width, cut), lambda i: (0, i)),
            pl.BlockSpec((cut, width), lambda i: (i, 0)),
            pl.BlockSpec((cut,), lambda i: (i,)),
        ],
        out_specs=[VMEM] * 4
        + [pl.BlockSpec((width // 2, cut), lambda i: (0, i))] * 4
        + [pl.BlockSpec((cut,), lambda i: (i,))],
        scratch_shapes=[pltpu.VMEM((2 * rows, width), f32)] * 2
        + [pltpu.VMEM((width, cut), bf16)] * 2
        + [pltpu.VMEM((2 * rows, width), bf16)] * 2,
        **params(48),
    )(me_s, mlp_low, mlp_oth, g_own, g_oth, w_up, w_down, up_bias)
    gmi_got = lax.ppermute(gmi_send, "heads", SWAP)

    def take(keep, send, offsets):
        if block % 16 == 0:
            return keep, send
        total = jnp.concatenate([keep, send], axis=0).reshape(count, block, -1)
        total = arrange(total, offsets, me).reshape(width, -1)
        return total[: width // 2], total[width // 2 :]

    up_keep, up_send = take(up_keep, up_send, slots_a)
    down_keep, down_send = take(down_keep, down_send, slots_b)
    up_got = exchange(up_send, order_a[0], count)
    down_got = exchange(down_send, order_b[0], count)

    grad_resid, gc_own, gc_oth, wo_keep, wo_send, sums_mid = call(
        functools.partial(middle_kernel, n, seq, half, block, slots_b),
        "middle",
        [
            ((rows, width), f32),
            ((n, seq, half), bf16),
            ((n, seq, half), bf16),
            *[((width, half) if block % 16 == 0 else (half, width), bf16)] * 2,
            ((8, width), f32),
        ],
        [((width, width), f32), ((width, half), f32)],
        [me_s, head_s],
        [gmi_own, gmi_got, resid, g_own, mlp_gain, w_out, ctx_own, ctx_oth],
        28,
    )
    if block % 16:
        wo = jnp.concatenate([wo_keep, wo_send], axis=0).reshape(count, 2, block // 2, 2, half)
        wo = arrange(wo, slots_b, me).swapaxes(2, 3)
        wo_keep = lax.dynamic_index_in_dim(wo, head, 1, keepdims=False).reshape(width, half)
        wo_send = lax.dynamic_index_in_dim(wo, 1 - head, 1, keepdims=False).reshape(width, half)
    wo_got = lax.ppermute(wo_send, "heads", SWAP)

    def back(name, qkv, gc, lse, fused, kinds, more):
        wide = width if fused else half
        return call(
            functools.partial(back_kernel, n, seq, half, block, (slots_a, slots_b), fused),
            name,
            [
                ((rows, 3 * half), bf16),
                *[((width // 2, 2 * half), k) for k in kinds],
                *[((width // 2, wide), k) for k in kinds],
                ((8, half), f32),
            ],
            [((rows, 3 * half), f32), ((width, 2 * half), kinds[0]), ((width, half), kinds[0])],
            [lens, me_s],
            [qkv, gc, lse, normed, *more],
            32,
        )

    dq_oth, *dw_oth, sums_oth = back("back_other", qkv_oth, gc_oth, lse_oth, False, (bf16, bf16), [])
    dw_got = [lax.ppermute(d, "heads", SWAP) for d in dw_oth]
    (up, down), (up_send, down_send), _ = combine(
        "add_first", [(up_keep, up_got, 0), (down_keep, down_got, 0)], [[0], [1]]
    )
    qkv_own, up_send, down_send = tie((qkv_own, up_send, down_send))
    up_got = exchange(up_send, order_a[1], count)
    down_got = exchange(down_send, order_b[1], count)
    if block % 16:
        dq_own, *dw_own, sums_own = back("back_own", qkv_own, gc_own, lse_own, False, (f32, f32), [])
        qk_keep, qk_send, v_keep, v_send = [d + o.astype(f32) for d, o in zip(dw_own, dw_got)]
        qk_keep, qk_send = take(qk_keep, qk_send, slots_a)
        v_keep, v_send = take(v_keep, v_send, slots_b)
        wo = wo_keep.astype(f32) + wo_got.astype(f32)
        vo_keep = jnp.concatenate([v_keep, wo[: width // 2]], axis=1)
        vo_send = jnp.concatenate([v_send, wo[width // 2 :]], axis=1).astype(bf16)
        qk_send = qk_send.astype(bf16)
    else:
        dq_own, qk_keep, qk_send, vo_keep, vo_send, sums_own = back(
            "back_own", qkv_own, gc_own, lse_own, True, (f32, bf16), [*dw_got, wo_keep, wo_got]
        )
    (up, down), (wide_send,), _ = combine("add_second", [(up, up_got, 0), (down, down_got, 0)], [[0, 1]])
    qk_send, vo_send, wide_send, dq_own = tie((qk_send, vo_send, wide_send, dq_own))
    qk_got = exchange(qk_send, order_a[0], count)
    vo_got = exchange(vo_send, order_b[0], count)
    wide_got = exchange(wide_send, order_a[2], count)
    grad_tok, vecs = call(
        functools.partial(last_kernel, half),
        "last",
        [((rows, width), f32), ((8, max(2 * width, hidden)), f32)],
        [],
        [head_s],
        [dq_own, dq_oth, w_qkv, w_oth, tok, attn_gain, grad_resid, sums_mid, sums_own, sums_oth, up_sums],
        24,
    )
    out_send, vecs = tie((out_send, vecs))
    out_got = lax.ppermute(out_send, "heads", SWAP)
    vecs = vecs + lax.ppermute(vecs, "heads", SWAP)
    vecs_got = exchange(vecs, order_a[0], count)
    layer_out = (resid + (out_own + out_got.astype(f32) + down_bias)).astype(bf16)
    qk_got, vo_got, wide_got, vecs_got = tie((qk_got, vo_got, wide_got, vecs_got))
    (qk, vo, up, down), (qk_send, vo_send, wide_send), (vecs,) = combine(
        "add_third",
        [(qk_keep, qk_got, 0), (vo_keep, vo_got, 0), (up, wide_got, 0), (down, wide_got, up.shape[0])],
        [[0], [1], [2, 3]],
        [(vecs, vecs_got, 0, False)],
    )
    qk_got = exchange(qk_send, order_a[1], count)
    vo_got = exchange(vo_send, order_b[1], count)
    wide_got = exchange(wide_send, order_a[3], count)
    vecs_got = exchange(vecs, order_a[1], count)
    qk_got, vo_got, wide_got, vecs_got = tie((qk_got, vo_got, wide_got, vecs_got))
    for mask in order_a[4:]:
        (up, down), (wide_send,), _ = combine(
            "add_more", [(up, wide_got, 0), (down, wide_got, up.shape[0])], [[0, 1]]
        )
        wide_got = exchange(wide_send, mask, count)
    (qk, vo), (pair_send,), (vecs,) = combine(
        "add_fourth", [(qk, qk_got, 0), (vo, vo_got, 0)], [[0, 1]], [(vecs, vecs_got, 0, False)]
    )
    for mask, later in zip(order_a[2:], order_a[3:]):
        pair_got, vecs_got = exchange(pair_send, mask, count), exchange(vecs, mask, count)
        if mask == order_a[2]:
            _, _, (grad_w_up, grad_w_down) = combine(
                "add_wide", [], [], [(up, wide_got, 0, False), (down, wide_got, up.shape[0], True)]
            )
        pair_got, vecs_got, grad_w_up = tie((pair_got, vecs_got, grad_w_up))
        (qk, vo), (pair_send,), (vecs,) = combine(
            "add_fifth",
            [(qk, pair_got, 0), (vo, pair_got, qk.shape[0])],
            [[0, 1]],
            [(vecs, vecs_got, 0, False)],
        )
    pair_got, vecs_got = exchange(pair_send, order_a[-1], count), exchange(vecs, order_a[-1], count)
    _, _, (qk, vo) = combine("add_last", [], [], [(qk, pair_got, 0, False), (vo, pair_got, qk.shape[0], False)])
    grad_w_qkv = jnp.stack([qk[:, :half], qk[:, half:], vo[:, :half]], axis=0)
    grad_w_out = jnp.concatenate([vo[: block // 2, half:], vo[block // 2 :, half:]], axis=1)
    part, up_part = width // count // 2, hidden // count
    piece = call(
        functools.partial(spread_kernel, count, width, hidden),
        "spread",
        [((part,), f32)] * 6 + [((2, part), f32), ((up_part,), f32)],
        [],
        [(me * 2 + head).reshape(1)],
        [vecs, vecs_got],
        8,
    )
    return (
        layer_out.reshape(n, seq, width),
        grad_tok.reshape(n, seq, width),
        piece[0],
        piece[1],
        grad_w_qkv,
        piece[6],
        grad_w_out,
        piece[4],
        piece[2],
        piece[3],
        grad_w_up,
        piece[7],
        grad_w_down,
        piece[5],
    )


def solution(mesh):
    in_specs = (
        P(("pairs", "heads"), None, None),
        P(("pairs", "heads"), None, None),
        P("pairs"),
        P(("pairs", "heads"), None),
        P(),
        P(),
        P(None, None, "heads"),
        P(None, "heads"),
        P(),
        P(),
        P(),
        P(),
        P(None, "heads"),
        P("heads"),
        P("heads", None),
        P(),
    )
    out_specs = (
        P(("pairs", "heads"), None, None),
        P(("pairs", "heads"), None, None),
        P(("pairs", "heads")),
        P(("pairs", "heads")),
        P(None, "pairs", "heads"),
        P(None, ("pairs", "heads")),
        P(("pairs", "heads"), None),
        P(("pairs", "heads")),
        P(("pairs", "heads")),
        P(("pairs", "heads")),
        P("pairs", "heads"),
        P(("pairs", "heads")),
        P("heads", "pairs"),
        P(("pairs", "heads")),
    )
    return jax.shard_map(
        per_device, mesh=mesh, in_specs=in_specs, out_specs=out_specs, check_vma=False
    )
```

time: 221 us -> 169 us (0.76)
  Pallas kernels: 91.8 us -> 76.7 us
  starting transfers between devices: 38.5 us -> 23.8 us
  waiting for transfers between devices: 65 us -> 50.5 us
  local copies, waits for them, and re-layouts: 14.9 us -> 10.9 us
  other arithmetic: 9.34 us -> 6.19 us
    ppermute x24 -> x16, waiting for transfers between devices: 60.9 us -> 43.9 us  [exchange(): return lax.ppermute(send, 'pairs', [(i, i ^ mask) for i in range(count)])]
    ppermute x24 -> x16, starting transfers between devices: 36 us -> 21.4 us  [exchange(): return lax.ppermute(send, 'pairs', [(i, i ^ mask) for i in range(count)])]
    pallas_call x6 -> x14, Pallas kernels: 60.3 us -> 49.5 us  [call(): pl.pallas_call(body, name=name, out_shape=[jax.ShapeDtypeStruct(s, d) for...]
    unnamed x47 -> x57, local copies, waits for them, and re-layouts: 3.13 us -> 10.7 us
    slice x31 -> x1, local copies, waits for them, and re-layouts: 6.37 us -> 0.01 us  [per_device(): vo[:block // 2, half:]]
    pallas_call x1, Pallas kernels: 31.6 us -> 27.2 us  [per_device(): pl.pallas_call(functools.partial(mlp_kernel, steps, (slots_a, slots_b), b...]
    reshape x14 -> x0, local copies, waits for them, and re-layouts: 4.22 us -> none  [the longest x6 3.52 us: per_device(): row = lambda v: v.reshape(1, -1)]
  transfers between devices with their start and end apart: 33 -> 28, of which waited for: 22 -> 12; matrix products, arithmetic and copies ran while one was open for 8% -> 3% of each run, Pallas kernels for 10% -> 29%
where the time goes in v2:
time: 169 us
  Pallas kernels  76.7 us (45%)
  waiting for transfers between devices  50.5 us (30%)
  starting transfers between devices  23.8 us (14%)
  local copies, waits for them, and re-layouts  10.9 us (6%)
  other arithmetic  6.19 us (4%)
    pallas_call x14, Pallas kernels, call(): pl.pallas_call(body, name=name, out_shape=[jax.ShapeDtypeStruct(s, d) for...  49.5 us
    ppermute x16, waiting for transfers between devices, exchange(): return lax.ppermute(send, 'pairs', [(i, i ^ mask) for i in range(count)])  43.9 us
    pallas_call x1, Pallas kernels, per_device(): pl.pallas_call(functools.partial(mlp_kernel, steps, (slots_a, slots_b), b...  27.2 us
    ppermute x16, starting transfers between devices, exchange(): return lax.ppermute(send, 'pairs', [(i, i ^ mask) for i in range(count)])  21.4 us
    unnamed x57, local copies, waits for them, and re-layouts  10.7 us
  transfers between devices with their start and end apart: 28, of which 12 were waited for; matrix products, arithmetic and copies ran while one was open for 3% of the time, Pallas kernels for 29%

profile of v2, /device:TPU:0, one launch (start us, length us, event | category | flops | bytes accessed | tf_op | source)
XLA Modules:
  0.0 169.0 jit_solution(3523993521298804213)
XLA Ops:
  0.7 0.5 collective-permute-start
  1.2 0.1 collective-permute-start.1
  1.3 0.7 convert_element_type.9
  2.0 1.3 broadcast_multiply_fusion
  3.3 0.5 collective-permute-start.3
  3.9 1.5 copy-done.1
  5.4 8.1 %attend_own.1 = (bf16[560,768]{1,0:T(8,128)(2,1)S(1)}, bf16[2,280,1152]{2,1,0:T(8,128)(2,1)S(1)}, bf16[560,384]{1,0:T(8,128)(2,1)S(1)}, f32[2,8,280]{2,1,0:T(8,128)S(1)}) custom-call(s32[2]{0:T(128)S(1)} %dynamic_slice.3.len_ref, bf16[560,768]{1,0:T(8,128)(2,1)S(1)} %bitcast.13, f32[768]{0:T(1024)S(1)} %copy-done.19, f32[768]{0:T(1024)S(1)} %copy-done.21, ...), custom_call_target="tpu_custom_call" | custom-call | bytes 1048576 | tf_op jit(solution)/shard_map/attend_own/pallas_call | solution.py:374
  13.5 1.1 copy-done.9
  14.6 11.0 %attend_other.1 = (bf16[2,280,1152]{2,1,0:T(8,128)(2,1)S(1)}, bf16[560,384]{1,0:T(8,128)(2,1)S(1)}, f32[2,8,280]{2,1,0:T(8,128)S(1)}, f32[560,768]{1,0:T(8,128)S(1)}, bf16[560,768]{1,0:T(8,128)(2,1)}) custom-call(s32[2]{0:T(128)S(1)} %dynamic_slice.3.len_ref, s32[1]{0:T(128)} %bitcast.head_ref, bf16[560,768]{1,0:T(8,128)(2,1)S(1)} %get-tuple-element.107.normed, ...), custom_call_target="tpu_custom_call" | custom-call | bytes 1048576 | tf_op jit(solution)/shard_map/attend_other/pallas_call | solution.py:374
  25.5 1.2 copy-done.3
  26.7 1.2 copy-done.11
  27.9 0.1 collective-permute-start.2
  28.0 2.6 %collective-permute-done.2.a_oth = bf16[560,768]{1,0:T(8,128)(2,1)} collective-permute-done((bf16[560,768]{1,0:T(8,128)(2,1)}, bf16[560,768]{1,0:T(8,128)(2,1)}, u32[]{:S(2)}, u32[]{:S(2)}) %collective-permute-start.2) | collective-permute-done | bytes 860192 | tf_op jit(solution)/shard_map/ppermute | solution.py:450
  30.6 27.2 %mlp.1 = (f32[560,768]{1,0:T(8,128)}, bf16[560,768]{1,0:T(8,128)(2,1)}, f32[560,768]{1,0:T(8,128)}, bf16[560,768]{1,0:T(8,128)(2,1)S(1)}, bf16[384,1536]{1,0:T(8...) custom-call(s32[1]{0:T(128)} %bitcast.2.me_ref, ...), custom_call_target="tpu_custom_call" | custom-call | bytes 1048576 | tf_op jit(solution)/shard_map/mlp/pallas_call | solution.py:454
  57.9 2.7 %collective-permute-start.4 = (bf16[384,1536]{1,0:T(8,128)(2,1)}, bf16[384,1536]{1,0:T(8,128)(2,1)S(1)}, u32[]{:S(2)}, u32[]{:S(2)}) collective-permute-start(bf16[384,1536]{1,0:T(8,128)(2,1)} %get-tuple-element.115), channel_id=1, source_target_pairs={{0,2},{2,0},{4,6},{6,4},{8,10},{10,8},{12,14},{14,12},{16,18},{18,... | collective-permute-start | bytes 3538952 | tf_op jit(solution)/shard_map/ppermute | solution.py:397
  60.5 1.5 collective-permute-start.5
  62.0 2.4 %collective-permute-done.6.gmi_got = bf16[560,768]{1,0:T(8,128)(2,1)S(1)} collective-permute-done((bf16[560,768]{1,0:T(8,128)(2,1)S(1)}, bf16[560,768]{1,0:T(8,128)(2,1)S(1)}, u32[]{:S(2)}, u32[]{:S(2)}) %collective-permute-start.6) | collective-permute-done | bytes 860192 | tf_op jit(solution)/shard_map/ppermute | solution.py:481
  64.4 1.5 copy-done.8
  65.9 3.5 %middle.1 = (f32[560,768]{1,0:T(8,128)S(1)}, bf16[2,280,384]{2,1,0:T(8,128)(2,1)S(1)}, bf16[2,280,384]{2,1,0:T(8,128)(2,1)S(1)}, bf16[768,384]{1,0:T(8,128)(2,1)...) custom-call(s32[1]{0:T(128)} %bitcast.2.me_ref, s32[1]{0:T(128)} %bitcast.head_ref, f32[560,768]{1,0:T(8,128)S(1)} %copy-done.8, ...), custom_call_target="tpu_custom_call" | custom-call | bytes 1048576 | tf_op jit(solution)/shard_map/middle/pallas_call | solution.py:374
  69.5 7.9 %back_other.1 = (bf16[560,1152]{1,0:T(8,128)(2,1)S(1)}, bf16[384,768]{1,0:T(8,128)(2,1)S(1)}, bf16[384,768]{1,0:T(8,128)(2,1)S(1)}, bf16[384,384]{1,0:T(8,128)(2...) custom-call(s32[2]{0:T(128)S(1)} %dynamic_slice.3.len_ref, s32[1]{0:T(128)} %bitcast.2.me_ref, ...), custom_call_target="tpu_custom_call" | custom-call | bytes 1048576 | tf_op jit(solution)/shard_map/back_other/pallas_call | solution.py:374
  77.3 0.2 collective-permute-start.10
  77.5 0.4 collective-permute-start.9
  77.9 0.1 collective-permute-start.7
  78.1 9.2 %collective-permute-done.4.refs_1_ = bf16[384,1536]{1,0:T(8,128)(2,1)S(1)} collective-permute-done((bf16[384,1536]{1,0:T(8,128)(2,1)}, bf16[384,1536]{1,0:T(8,128)(2,1)S(1)}, u32[]{:S(2)}, u32[]{:S(2)}) %collective-permute-start.4) | collective-permute-done | bytes 1179680 | tf_op jit(solution)/shard_map/ppermute | solution.py:397
  87.2 1.5 collective-permute-done.5.refs_3_
  88.7 0.5 add_first.1
  89.2 1.6 collective-permute-start.12
  90.8 0.8 collective-permute-start.13
  91.6 8.1 %back_own.1 = (bf16[560,1152]{1,0:T(8,128)(2,1)S(1)}, f32[384,768]{1,0:T(8,128)S(1)}, bf16[384,768]{1,0:T(8,128)(2,1)S(1)}, f32[384,768]{1,0:T(8,128)S(1)}, bf16...) custom-call(s32[2]{0:T(128)S(1)} %dynamic_slice.3.len_ref, s32[1]{0:T(128)} %bitcast.2.me_ref, ...), custom_call_target="tpu_custom_call" | custom-call | bytes 1048576 | tf_op jit(solution)/shard_map/back_own/pallas_call | solution.py:374
  99.7 5.3 %collective-permute-done.12.refs_1_ = bf16[192,1536]{1,0:T(8,128)(2,1)S(1)} collective-permute-done((bf16[192,1536]{1,0:T(8,128)(2,1)S(1)}, bf16[192,1536]{1,0:T(8,128)(2,1)S(1)}, u32[]{:S(2)}, u32[]{:S(2)}) %collective-permute-start.12) | collective-permute-done | bytes 589856 | tf_op jit(solution)/shard_map/ppermute | solution.py:397
  105.0 1.2 collective-permute-done.13.refs_3_
  106.2 0.3 add_second.1
  106.5 0.6 collective-permute-start.15
  107.1 0.4 collective-permute-start.16
  107.5 1.7 %collective-permute-start.17 = (bf16[192,1536]{1,0:T(8,128)(2,1)S(1)}, bf16[192,1536]{1,0:T(8,128)(2,1)S(1)}, u32[]{:S(2)}, u32[]{:S(2)}) collective-permute-start(bf16[192,1536]{1,0:T(8,128)(2,1)S(1)} %get-tuple-element.156), channel_id=1, source_target_pairs={{0,8},{2,10},{4,12},{6,14},{8,0},{10,2},{12,4},{14,6},{16,24},{18,... | collective-permute-start | bytes 1769480 | tf_op jit(solution)/shard_map/ppermute | solution.py:397
  109.2 6.4 %last.1 = (f32[560,768]{1,0:T(8,128)}, f32[8,1536]{1,0:T(8,128)S(1)}) custom-call(s32[1]{0:T(128)} %bitcast.head_ref, bf16[560,1152]{1,0:T(8,128)(2,1)S(1)} %get-tuple-element.143.dq_own, bf16[560,1152]{1,0:T(8,128)(2,1)S(1)} %get-tuple-element.144.dq_oth, bf16[3,768,384]{2,1,0:T(8,128)(2,1)S(1)} %copy-done.2, ...), custom_call_target="tpu_custom_call" | custom-call | bytes 1048576 | tf_op jit(solution)/shard_map/last/pallas_call | solution.py:374
  115.6 0.5 collective-permute-start.18
  116.1 1.6 collective-permute-done.18
  117.6 1.5 collective-permute-start.19
  119.1 3.1 %collective-permute-done.19.refs_8_ = f32[8,1536]{1,0:T(8,128)S(1)} collective-permute-done((f32[8,1536]{1,0:T(8,128)S(1)}, f32[8,1536]{1,0:T(8,128)S(1)}, u32[]{:S(2)}, u32[]{:S(2)}) %collective-permute-start.19) | collective-permute-done | bytes 49184 | tf_op jit(solution)/shard_map/ppermute | solution.py:397
  122.3 0.4 add_third.1
  122.7 1.1 collective-permute-start.20
  123.8 1.5 collective-permute-start.21
  125.2 2.6 %collective-permute-start.22 = (bf16[96,1536]{1,0:T(8,128)(2,1)S(1)}, bf16[96,1536]{1,0:T(8,128)(2,1)S(1)}, u32[]{:S(2)}, u32[]{:S(2)}) collective-permute-start(bf16[96,1536]{1,0:T(8,128)(2,1)S(1)} %get-tuple-element.168), channel_id=1, source_target_pairs={{0,16},{2,18},{4,20},{6,22},{8,24},{10,26},{12,28},{14,30},{16,0},... | collective-permute-start | bytes 884744 | tf_op jit(solution)/shard_map/ppermute | solution.py:397
  127.9 0.5 collective-permute-start.23
  128.3 4.0 %collective-permute-done.23.refs_5_ = f32[8,1536]{1,0:T(8,128)S(1)} collective-permute-done((f32[8,1536]{1,0:T(8,128)S(1)}, f32[8,1536]{1,0:T(8,128)S(1)}, u32[]{:S(2)}, u32[]{:S(2)}) %collective-permute-start.23) | collective-permute-done | bytes 49184 | tf_op jit(solution)/shard_map/ppermute | solution.py:397
  132.4 7.9 %collective-permute-done.22.refs_1_ = bf16[96,1536]{1,0:T(8,128)(2,1)S(1)} collective-permute-done((bf16[96,1536]{1,0:T(8,128)(2,1)S(1)}, bf16[96,1536]{1,0:T(8,128)(2,1)S(1)}, u32[]{:S(2)}, u32[]{:S(2)}) %collective-permute-start.22) | collective-permute-done | bytes 294944 | tf_op jit(solution)/shard_map/ppermute | solution.py:397
  140.3 0.8 add_fourth.1
  141.1 0.7 copy-done.15
  141.8 0.7 copy-done.17
  142.5 2.0 %collective-permute-start.25 = (f32[8,1536]{1,0:T(8,128)S(1)}, f32[8,1536]{1,0:T(8,128)S(1)}, u32[]{:S(2)}, u32[]{:S(2)}) collective-permute-start(f32[8,1536]{1,0:T(8,128)S(1)} %get-tuple-element.176.refs_3_), channel_id=1, source_target_pairs={{0,8},{2,10},{4,12},{6,14},{8,0},{10,2},{12,4},{14,6},{16,24},{18,... | collective-permute-start | bytes 147464 | tf_op jit(solution)/shard_map/ppermute | solution.py:397
  144.6 1.0 add_wide.1
  145.5 7.2 %collective-permute-done.25.refs_4_ = f32[8,1536]{1,0:T(8,128)S(1)} collective-permute-done((f32[8,1536]{1,0:T(8,128)S(1)}, f32[8,1536]{1,0:T(8,128)S(1)}, u32[]{:S(2)}, u32[]{:S(2)}) %collective-permute-start.25) | collective-permute-done | bytes 49184 | tf_op jit(solution)/shard_map/ppermute | solution.py:397
  152.7 1.0 copy-done.16
  153.7 1.0 copy-done.18
  154.7 1.0 add_fifth.1
  155.7 0.4 collective-permute-start.27
  156.0 2.6 %collective-permute-start.26 = (f32[8,1536]{1,0:T(8,128)S(1)}, f32[8,1536]{1,0:T(8,128)S(1)}, u32[]{:S(2)}, u32[]{:S(2)}) collective-permute-start(f32[8,1536]{1,0:T(8,128)S(1)} %get-tuple-element.184.vec), channel_id=1, source_target_pairs={{0,16},{2,18},{4,20},{6,22},{8,24},{10,26},{12,28},{14,30},{16,0},... | collective-permute-start | bytes 147464 | tf_op jit(solution)/shard_map/ppermute | solution.py:397
  158.7 2.9 %add_convert_fusion = bf16[560,768]{1,0:T(8,128)(2,1)} fusion(f32[560,768]{1,0:T(8,128)S(1)} %copy-done.5, f32[560,768]{1,0:T(8,128)} %get-tuple-element.111, bf16[560,768]{1,0:T(8,128)(2,1)} %collective-permute-done.14, f32[768]{0:T(1024)S(1)} %copy-done.26), kind=kLoop, calls=%fused_computation | loop fusion | flops 2150400 | bytes 5164032 | tf_op jit(solution)/shard_map/convert_element_type | solution.py:573
  161.5 1.0 copy.30
  162.5 4.4 %collective-permute-done.26.vec_got = f32[8,1536]{1,0:T(8,128)S(1)} collective-permute-done((f32[8,1536]{1,0:T(8,128)S(1)}, f32[8,1536]{1,0:T(8,128)S(1)}, u32[]{:S(2)}, u32[]{:S(2)}) %collective-permute-start.26) | collective-permute-done | bytes 49184 | tf_op jit(solution)/shard_map/ppermute | solution.py:397
  166.9 0.7 spread.1
  167.7 0.6 pad_maximum_fusion.1
  168.3 0.7 pad_maximum_fusion
  (75 shorter events, 0.3 us)
Async XLA Ops:
  0.6 3.3 %copy-start.25 = (f32[2,384]{1,0:T(2,128)S(1)}, f32[2,384]{1,0:T(2,128)}, u32[]{:S(2)}) copy-start(f32[2,384]{1,0:T(2,128)} %bias.2) | copy-start | bytes 9220
  0.7 3.2 %copy-start.27 = (s32[4]{0:T(128)S(1)}, s32[4]{0:T(128)}, u32[]{:S(2)}) copy-start(s32[4]{0:T(128)} %param.18) | copy-start | bytes 52
  0.7 3.2 %copy-start = (bf16[2,280,768]{2,1,0:T(8,128)(2,1)S(1)}, bf16[2,280,768]{2,1,0:T(8,128)(2,1)}, u32[]{:S(2)}) copy-start(bf16[2,280,768]{2,1,0:T(8,128)(2,1)} %param.16) | copy-start | bytes 2580484
  0.7 3.2 %copy-start.19 = (f32[768]{0:T(1024)S(1)}, f32[768]{0:T(1024)}, u32[]{:S(2)}) copy-start(f32[768]{0:T(1024)} %gain.7) | copy-start | bytes 9220
  0.7 3.2 %copy-start.21 = (f32[768]{0:T(1024)S(1)}, f32[768]{0:T(1024)}, u32[]{:S(2)}) copy-start(f32[768]{0:T(1024)} %shift.2) | copy-start | bytes 9220
  0.7 13.8 %collective-permute-start = (bf16[3,768,384]{2,1,0:T(8,128)(2,1)}, bf16[3,768,384]{2,1,0:T(8,128)(2,1)}, u32[]{:S(2)}, u32[]{:S(2)}) collective-permute-start(bf16[3,768,384]{2,1,0:T(8,128)(2,1)} %w_own.1), channel_id=1, source_target_pairs={{0,1},{1,0},{2,3},{3,2},{4,5},{5,4},{6,7},{7,6},{8,9},{9,8},{10,11... | collective-permute-start | bytes 5308424 | tf_op jit(solution)/shard_map/ppermute | solution.py:421
  1.2 13.3 %collective-permute-start.1 = (f32[2,384]{1,0:T(2,128)}, f32[2,384]{1,0:T(2,128)S(1)}, u32[]{:S(2)}, u32[]{:S(2)}) collective-permute-start(f32[2,384]{1,0:T(2,128)} %bias.2), channel_id=1, source_target_pairs={{0,1},{1,0},{2,3},{3,2},{4,5},{5,4},{6,7},{7,6},{8,9},{9,8},{10,11... | collective-permute-start | bytes 9224 | tf_op jit(solution)/shard_map/ppermute | solution.py:422
  3.3 11.2 %copy-start.20 = (f32[768]{0:T(1024)S(1)}, f32[768]{0:T(1024)}, u32[]{:S(2)}) copy-start(f32[768]{0:T(1024)} %gain.6) | copy-start | bytes 9220
  3.3 11.2 %copy-start.23 = (f32[768]{0:T(1024)S(1)}, f32[768]{0:T(1024)}, u32[]{:S(2)}) copy-start(f32[768]{0:T(1024)} %out_bias.1) | copy-start | bytes 9220
  3.3 11.2 %copy-start.24 = (f32[768]{0:T(1024)S(1)}, f32[768]{0:T(1024)}, u32[]{:S(2)}) copy-start(f32[768]{0:T(1024)} %shift.3) | copy-start | bytes 9220
  3.3 24.7 %collective-permute-start.3 = (bf16[560,768]{1,0:T(8,128)(2,1)S(1)}, bf16[560,768]{1,0:T(8,128)(2,1)}, u32[]{:S(2)}, u32[]{:S(2)}) collective-permute-start(bf16[560,768]{1,0:T(8,128)(2,1)S(1)} %bitcast.16), channel_id=1, source_target_pairs={{0,1},{1,0},{2,3},{3,2},{4,5},{5,4},{6,7},{7,6},{8,9},{9,8},{10,11... | collective-permute-start | bytes 2580488 | tf_op jit(solution)/shard_map/ppermute | solution.py:427
  3.9 1.5 copy-start.1
  5.4 9.2 %copy-start.6 = (bf16[768,768]{1,0:T(8,128)(2,1)S(1)}, bf16[768,768]{1,0:T(8,128)(2,1)}, u32[]{:S(2)}) copy-start(bf16[768,768]{1,0:T(8,128)(2,1)} %w_out.3) | copy-start | bytes 3538948
  13.5 1.1 copy-start.9
  14.6 16.1 %copy-start.22 = (bf16[1536]{0:T(1024)(128)(2,1)S(1)}, bf16[1536]{0:T(1024)(128)(2,1)}, u32[]{:S(2)}) copy-start(bf16[1536]{0:T(1024)(128)(2,1)} %bias.3) | copy-start | bytes 9220
  25.5 1.2 copy-start.3
  26.7 1.2 copy-start.11
  27.9 2.7 %collective-permute-start.2 = (bf16[560,768]{1,0:T(8,128)(2,1)}, bf16[560,768]{1,0:T(8,128)(2,1)}, u32[]{:S(2)}, u32[]{:S(2)}) collective-permute-start(bf16[560,768]{1,0:T(8,128)(2,1)} %get-tuple-element.110.a_own), channel_id=1, source_target_pairs={{0,1},{1,0},{2,3},{3,2},{4,5},{5,4},{6,7},{7,6},{8,9},{9,8},{10,11... | collective-permute-start | bytes 2580488 | tf_op jit(solution)/shard_map/ppermute | solution.py:450
  30.6 33.8 %copy-start.4 = (f32[560,768]{1,0:T(8,128)S(1)}, f32[560,768]{1,0:T(8,128)}, u32[]{:S(2)}) copy-start(f32[560,768]{1,0:T(8,128)} %copy-done.3) | copy-start | bytes 5160964
  30.6 33.8 %copy-start.7 = (bf16[768,768]{1,0:T(8,128)(2,1)S(1)}, bf16[768,768]{1,0:T(8,128)(2,1)}, u32[]{:S(2)}) copy-start(bf16[768,768]{1,0:T(8,128)(2,1)} %w_out.3) | copy-start | bytes 3538948
  57.9 29.4 %collective-permute-start.4 = (bf16[384,1536]{1,0:T(8,128)(2,1)}, bf16[384,1536]{1,0:T(8,128)(2,1)S(1)}, u32[]{:S(2)}, u32[]{:S(2)}) collective-permute-start(bf16[384,1536]{1,0:T(8,128)(2,1)} %get-tuple-element.115), channel_id=1, source_target_pairs={{0,2},{2,0},{4,6},{6,4},{8,10},{10,8},{12,14},{14,12},{16,18},{18,... | collective-permute-start | bytes 3538952 | tf_op jit(solution)/shard_map/ppermute | solution.py:397
  60.5 28.2 %collective-permute-start.5 = (bf16[384,1536]{1,0:T(8,128)(2,1)}, bf16[384,1536]{1,0:T(8,128)(2,1)S(1)}, u32[]{:S(2)}, u32[]{:S(2)}) collective-permute-start(bf16[384,1536]{1,0:T(8,128)(2,1)} %get-tuple-element.117), channel_id=1, source_target_pairs={{0,4},{2,6},{4,0},{6,2},{8,12},{10,14},{12,8},{14,10},{16,20},{18,... | collective-permute-start | bytes 3538952 | tf_op jit(solution)/shard_map/ppermute | solution.py:397
  62.0 2.4 %collective-permute-start.6 = (bf16[560,768]{1,0:T(8,128)(2,1)S(1)}, bf16[560,768]{1,0:T(8,128)(2,1)S(1)}, u32[]{:S(2)}, u32[]{:S(2)}) collective-permute-start(bf16[560,768]{1,0:T(8,128)(2,1)S(1)} %get-tuple-element.122), channel_id=1, source_target_pairs={{0,1},{1,0},{2,3},{3,2},{4,5},{5,4},{6,7},{7,6},{8,9},{9,8},{10,11... | collective-permute-start | bytes 2580488 | tf_op jit(solution)/shard_map/ppermute | solution.py:481
  64.4 1.5 copy-start.8
  65.9 3.6 %copy-start.12 = (bf16[2,280,1152]{2,1,0:T(8,128)(2,1)S(1)}, bf16[2,280,1152]{2,1,0:T(8,128)(2,1)}, u32[]{:S(2)}) copy-start(bf16[2,280,1152]{2,1,0:T(8,128)(2,1)} %copy-done.11) | copy-start | bytes 3870724
  69.4 19.2 %copy-start.13 = (bf16[384,1536]{1,0:T(8,128)(2,1)S(1)}, bf16[384,1536]{1,0:T(8,128)(2,1)}, u32[]{:S(2)}) copy-start(bf16[384,1536]{1,0:T(8,128)(2,1)} %get-tuple-element.114.refs_0_) | copy-start | bytes 3538948
  69.5 19.2 %copy-start.14 = (bf16[384,1536]{1,0:T(8,128)(2,1)S(1)}, bf16[384,1536]{1,0:T(8,128)(2,1)}, u32[]{:S(2)}) copy-start(bf16[384,1536]{1,0:T(8,128)(2,1)} %get-tuple-element.116.refs_2_) | copy-start | bytes 3538948
  77.3 11.9 %collective-permute-start.10 = (bf16[384,384]{1,0:T(8,128)(2,1)S(1)}, bf16[384,384]{1,0:T(8,128)(2,1)S(1)}, u32[]{:S(2)}, u32[]{:S(2)}) collective-permute-start(bf16[384,384]{1,0:T(8,128)(2,1)S(1)} %get-tuple-element.132), channel_id=1, source_target_pairs={{0,1},{1,0},{2,3},{3,2},{4,5},{5,4},{6,7},{7,6},{8,9},{9,8},{10,11... | collective-permute-start | bytes 884744 | tf_op jit(solution)/shard_map/ppermute | solution.py:535
  77.5 13.3 %collective-permute-start.9 = (bf16[384,384]{1,0:T(8,128)(2,1)S(1)}, bf16[384,384]{1,0:T(8,128)(2,1)S(1)}, u32[]{:S(2)}, u32[]{:S(2)}) collective-permute-start(bf16[384,384]{1,0:T(8,128)(2,1)S(1)} %get-tuple-element.131), channel_id=1, source_target_pairs={{0,1},{1,0},{2,3},{3,2},{4,5},{5,4},{6,7},{7,6},{8,9},{9,8},{10,11... | collective-permute-start | bytes 884744 | tf_op jit(solution)/shard_map/ppermute | solution.py:535
  77.9 13.7 %collective-permute-start.7 = (bf16[384,768]{1,0:T(8,128)(2,1)S(1)}, bf16[384,768]{1,0:T(8,128)(2,1)S(1)}, u32[]{:S(2)}, u32[]{:S(2)}) collective-permute-start(bf16[384,768]{1,0:T(8,128)(2,1)S(1)} %get-tuple-element.129), channel_id=1, source_target_pairs={{0,1},{1,0},{2,3},{3,2},{4,5},{5,4},{6,7},{7,6},{8,9},{9,8},{10,11... | collective-permute-start | bytes 1769480 | tf_op jit(solution)/shard_map/ppermute | solution.py:535
  87.2 4.4 %collective-permute-start.8 = (bf16[384,768]{1,0:T(8,128)(2,1)S(1)}, bf16[384,768]{1,0:T(8,128)(2,1)S(1)}, u32[]{:S(2)}, u32[]{:S(2)}) collective-permute-start(bf16[384,768]{1,0:T(8,128)(2,1)S(1)} %get-tuple-element.130), channel_id=1, source_target_pairs={{0,1},{1,0},{2,3},{3,2},{4,5},{5,4},{6,7},{7,6},{8,9},{9,8},{10,11... | collective-permute-start | bytes 1769480 | tf_op jit(solution)/shard_map/ppermute | solution.py:535
  88.7 2.9 %collective-permute-start.11 = (bf16[768,384]{1,0:T(8,128)(2,1)S(1)}, bf16[768,384]{1,0:T(8,128)(2,1)S(1)}, u32[]{:S(2)}, u32[]{:S(2)}) collective-permute-start(bf16[768,384]{1,0:T(8,128)(2,1)S(1)} %get-tuple-element.134), channel_id=1, source_target_pairs={{0,1},{1,0},{2,3},{3,2},{4,5},{5,4},{6,7},{7,6},{8,9},{9,8},{10,11... | collective-permute-start | bytes 1769480 | tf_op jit(solution)/shard_map/ppermute | solution.py:515
  88.7 2.9 %copy-start.10 = (bf16[2,280,1152]{2,1,0:T(8,128)(2,1)S(1)}, bf16[2,280,1152]{2,1,0:T(8,128)(2,1)}, u32[]{:S(2)}) copy-start(bf16[2,280,1152]{2,1,0:T(8,128)(2,1)} %copy-done.9) | copy-start | bytes 3870724
  89.2 15.8 %collective-permute-start.12 = (bf16[192,1536]{1,0:T(8,128)(2,1)S(1)}, bf16[192,1536]{1,0:T(8,128)(2,1)S(1)}, u32[]{:S(2)}, u32[]{:S(2)}) collective-permute-start(bf16[192,1536]{1,0:T(8,128)(2,1)S(1)} %get-tuple-element.138), channel_id=1, source_target_pairs={{0,4},{2,6},{4,0},{6,2},{8,12},{10,14},{12,8},{14,10},{16,20},{18,... | collective-permute-start | bytes 1769480 | tf_op jit(solution)/shard_map/ppermute | solution.py:397
  90.8 15.4 %collective-permute-start.13 = (bf16[192,1536]{1,0:T(8,128)(2,1)S(1)}, bf16[192,1536]{1,0:T(8,128)(2,1)S(1)}, u32[]{:S(2)}, u32[]{:S(2)}) collective-permute-start(bf16[192,1536]{1,0:T(8,128)(2,1)S(1)} %get-tuple-element.140), channel_id=1, source_target_pairs={{0,2},{2,0},{4,6},{6,4},{8,10},{10,8},{12,14},{14,12},{16,18},{18,... | collective-permute-start | bytes 1769480 | tf_op jit(solution)/shard_map/ppermute | solution.py:397
  106.2 2.9 %copy-start.2 = (bf16[3,768,384]{2,1,0:T(8,128)(2,1)S(1)}, bf16[3,768,384]{2,1,0:T(8,128)(2,1)}, u32[]{:S(2)}) copy-start(bf16[3,768,384]{2,1,0:T(8,128)(2,1)} %w_own.1) | copy-start | bytes 5308420
  106.5 15.7 %collective-permute-start.15 = (bf16[384,768]{1,0:T(8,128)(2,1)S(1)}, bf16[384,768]{1,0:T(8,128)(2,1)S(1)}, u32[]{:S(2)}, u32[]{:S(2)}) collective-permute-start(bf16[384,768]{1,0:T(8,128)(2,1)S(1)} %get-tuple-element.154), channel_id=1, source_target_pairs={{0,2},{2,0},{4,6},{6,4},{8,10},{10,8},{12,14},{14,12},{16,18},{18,... | collective-permute-start | bytes 1769480 | tf_op jit(solution)/shard_map/ppermute | solution.py:397
  107.1 15.2 %collective-permute-start.16 = (bf16[384,768]{1,0:T(8,128)(2,1)S(1)}, bf16[384,768]{1,0:T(8,128)(2,1)S(1)}, u32[]{:S(2)}, u32[]{:S(2)}) collective-permute-start(bf16[384,768]{1,0:T(8,128)(2,1)S(1)} %get-tuple-element.155), channel_id=1, source_target_pairs={{0,4},{2,6},{4,0},{6,2},{8,12},{10,14},{12,8},{14,10},{16,20},{18,... | collective-permute-start | bytes 1769480 | tf_op jit(solution)/shard_map/ppermute | solution.py:397
  107.5 14.8 %collective-permute-start.17 = (bf16[192,1536]{1,0:T(8,128)(2,1)S(1)}, bf16[192,1536]{1,0:T(8,128)(2,1)S(1)}, u32[]{:S(2)}, u32[]{:S(2)}) collective-permute-start(bf16[192,1536]{1,0:T(8,128)(2,1)S(1)} %get-tuple-element.156), channel_id=1, source_target_pairs={{0,8},{2,10},{4,12},{6,14},{8,0},{10,2},{12,4},{14,6},{16,24},{18,... | collective-permute-start | bytes 1769480 | tf_op jit(solution)/shard_map/ppermute | solution.py:397
  115.6 43.1 %collective-permute-start.14 = (bf16[560,768]{1,0:T(8,128)(2,1)}, bf16[560,768]{1,0:T(8,128)(2,1)}, u32[]{:S(2)}, u32[]{:S(2)}) collective-permute-start(bf16[560,768]{1,0:T(8,128)(2,1)} %get-tuple-element.151), channel_id=1, source_target_pairs={{0,1},{1,0},{2,3},{3,2},{4,5},{5,4},{6,7},{7,6},{8,9},{9,8},{10,11... | collective-permute-start | bytes 2580488 | tf_op jit(solution)/shard_map/ppermute | solution.py:570
  115.6 2.1 %collective-permute-start.18 = (f32[8,1536]{1,0:T(8,128)S(1)}, f32[8,1536]{1,0:T(8,128)S(1)}, u32[]{:S(2)}, u32[]{:S(2)}) collective-permute-start(f32[8,1536]{1,0:T(8,128)S(1)} %get-tuple-element.157), channel_id=1, source_target_pairs={{0,1},{1,0},{2,3},{3,2},{4,5},{5,4},{6,7},{7,6},{8,9},{9,8},{10,11... | collective-permute-start | bytes 147464 | tf_op jit(solution)/shard_map/ppermute | solution.py:571
  117.6 4.6 %collective-permute-start.19 = (f32[8,1536]{1,0:T(8,128)S(1)}, f32[8,1536]{1,0:T(8,128)S(1)}, u32[]{:S(2)}, u32[]{:S(2)}) collective-permute-start(f32[8,1536]{1,0:T(8,128)S(1)} %add.31.refs_7_), channel_id=1, source_target_pairs={{0,2},{2,0},{4,6},{6,4},{8,10},{10,8},{12,14},{14,12},{16,18},{18,... | collective-permute-start | bytes 147464 | tf_op jit(solution)/shard_map/ppermute | solution.py:397
  122.7 9.7 %collective-permute-start.20 = (bf16[192,768]{1,0:T(8,128)(2,1)S(1)}, bf16[192,768]{1,0:T(8,128)(2,1)S(1)}, u32[]{:S(2)}, u32[]{:S(2)}) collective-permute-start(bf16[192,768]{1,0:T(8,128)(2,1)S(1)} %get-tuple-element.166), channel_id=1, source_target_pairs={{0,4},{2,6},{4,0},{6,2},{8,12},{10,14},{12,8},{14,10},{16,20},{18,... | collective-permute-start | bytes 884744 | tf_op jit(solution)/shard_map/ppermute | solution.py:397
  123.8 8.6 %collective-permute-start.21 = (bf16[192,768]{1,0:T(8,128)(2,1)S(1)}, bf16[192,768]{1,0:T(8,128)(2,1)S(1)}, u32[]{:S(2)}, u32[]{:S(2)}) collective-permute-start(bf16[192,768]{1,0:T(8,128)(2,1)S(1)} %get-tuple-element.167), channel_id=1, source_target_pairs={{0,2},{2,0},{4,6},{6,4},{8,10},{10,8},{12,14},{14,12},{16,18},{18,... | collective-permute-start | bytes 884744 | tf_op jit(solution)/shard_map/ppermute | solution.py:397
  125.2 15.0 %collective-permute-start.22 = (bf16[96,1536]{1,0:T(8,128)(2,1)S(1)}, bf16[96,1536]{1,0:T(8,128)(2,1)S(1)}, u32[]{:S(2)}, u32[]{:S(2)}) collective-permute-start(bf16[96,1536]{1,0:T(8,128)(2,1)S(1)} %get-tuple-element.168), channel_id=1, source_target_pairs={{0,16},{2,18},{4,20},{6,22},{8,24},{10,26},{12,28},{14,30},{16,0},... | collective-permute-start | bytes 884744 | tf_op jit(solution)/shard_map/ppermute | solution.py:397
  127.9 4.5 %collective-permute-start.23 = (f32[8,1536]{1,0:T(8,128)S(1)}, f32[8,1536]{1,0:T(8,128)S(1)}, u32[]{:S(2)}, u32[]{:S(2)}) collective-permute-start(f32[8,1536]{1,0:T(8,128)S(1)} %get-tuple-element.169.refs_4_), channel_id=1, source_target_pairs={{0,4},{2,6},{4,0},{6,2},{8,12},{10,14},{12,8},{14,10},{16,20},{18,... | collective-permute-start | bytes 147464 | tf_op jit(solution)/shard_map/ppermute | solution.py:397
  140.3 18.4 %copy-start.5 = (f32[560,768]{1,0:T(8,128)S(1)}, f32[560,768]{1,0:T(8,128)}, u32[]{:S(2)}) copy-start(f32[560,768]{1,0:T(8,128)} %copy-done.3) | copy-start | bytes 5160964
  140.3 18.4 %copy-start.26 = (f32[768]{0:T(1024)S(1)}, f32[768]{0:T(1024)}, u32[]{:S(2)}) copy-start(f32[768]{0:T(1024)} %param.31) | copy-start | bytes 9220
  141.1 0.7 copy-start.15
  141.8 0.7 copy-start.17
  142.5 10.2 %collective-permute-start.24 = (bf16[192,768]{1,0:T(8,128)(2,1)}, bf16[192,768]{1,0:T(8,128)(2,1)}, u32[]{:S(2)}, u32[]{:S(2)}) collective-permute-start(bf16[192,768]{1,0:T(8,128)(2,1)} %get-tuple-element.175), channel_id=1, source_target_pairs={{0,8},{2,10},{4,12},{6,14},{8,0},{10,2},{12,4},{14,6},{16,24},{18,... | collective-permute-start | bytes 884744 | tf_op jit(solution)/shard_map/ppermute | solution.py:397
  142.5 10.2 %collective-permute-start.25 = (f32[8,1536]{1,0:T(8,128)S(1)}, f32[8,1536]{1,0:T(8,128)S(1)}, u32[]{:S(2)}, u32[]{:S(2)}) collective-permute-start(f32[8,1536]{1,0:T(8,128)S(1)} %get-tuple-element.176.refs_3_), channel_id=1, source_target_pairs={{0,8},{2,10},{4,12},{6,14},{8,0},{10,2},{12,4},{14,6},{16,24},{18,... | collective-permute-start | bytes 147464 | tf_op jit(solution)/shard_map/ppermute | solution.py:397
  152.7 1.0 copy-start.16
  153.7 1.0 copy-start.18
  155.7 11.9 %collective-permute-start.27 = (bf16[96,768]{1,0:T(8,128)(2,1)S(1)}, bf16[96,768]{1,0:T(8,128)(2,1)S(1)}, u32[]{:S(2)}, u32[]{:S(2)}) collective-permute-start(bf16[96,768]{1,0:T(8,128)(2,1)S(1)} %get-tuple-element.188), channel_id=1, source_target_pairs={{0,16},{2,18},{4,20},{6,22},{8,24},{10,26},{12,28},{14,30},{16,0},... | collective-permute-start | bytes 442376 | tf_op jit(solution)/shard_map/ppermute | solution.py:397
  156.0 10.9 %collective-permute-start.26 = (f32[8,1536]{1,0:T(8,128)S(1)}, f32[8,1536]{1,0:T(8,128)S(1)}, u32[]{:S(2)}, u32[]{:S(2)}) collective-permute-start(f32[8,1536]{1,0:T(8,128)S(1)} %get-tuple-element.184.vec), channel_id=1, source_target_pairs={{0,16},{2,18},{4,20},{6,22},{8,24},{10,26},{12,28},{14,30},{16,0},... | collective-permute-start | bytes 147464 | tf_op jit(solution)/shard_map/ppermute | solution.py:397
